TPU v7x, 512 devices: a whole 4x8x8 slice. The times are simulated.
512 devices in a mesh: dp: 16 (over y, core), vocab: 32 (over z, x).
Axes of the slice: x: 4, y: 8, z: 8, core: 2. Of those that a mesh axis runs over, the one named last changes fastest.
Arguments:
- grad: bfloat16 [16, 4096, 3584], P('dp', 'vocab'), may hold values from -6 to 6
- error: float32 [16, 4096, 3584], P('dp', 'vocab'), may hold values from -4 to 4
- q_prev: float32 [3584, 32], replicated, may hold values from -0.09375 to 0.09375
Outputs:
- new_error: float32 [16, 4096, 3584], P('dp', 'vocab')
- p_basis: float32 [4096, 32], P('vocab')
- q_new: float32 [3584, 32], replicated
All inputs are finite; a program needn't handle non-finite values.
Results may differ from a plain program's by a relative error of at most 0.0003.
Values sent between devices are 32-bit elements; how exact they have to be, the bound alone decides.
No kernel may reach another device: no remote copies, remote signals or barrier semaphores. Data moves between devices by JAX's collectives and lax.ppermute only.
A program may use at most 64 MiB of HBM per device.

v0:
```python
import jax
import jax.numpy as jnp
from jax import lax
from jax.sharding import PartitionSpec as P


def reduce_right(product):
    return lax.psum(product, ("dp", "vocab"))


def right_solve(chol, values):
    return lax.linalg.triangular_solve(chol, values, left_side=False, lower=True, transpose_a=True)


def per_device(grad, error, q_prev):
    highest = lax.Precision.HIGHEST
    replicas = lax.axis_size("dp")
    merged = grad[0].astype(jnp.float32) + error[0]
    p_local = jnp.dot(merged, q_prev, precision=highest)
    p_sum = lax.psum(p_local, "dp")
    gram = lax.psum(jnp.dot(p_sum.T, p_sum, precision=highest), "vocab")
    chol = jnp.linalg.cholesky(gram)
    p_basis = right_solve(chol, p_sum)
    total = reduce_right(jnp.dot(merged.T, p_basis, precision=highest))
    q_new = total / replicas
    approx = jnp.dot(p_basis, q_new.T, precision=highest)
    new_error = merged - approx
    return (new_error[None], p_basis, q_new)


def solution(mesh):
    placed = (P("dp", "vocab", None), P("dp", "vocab", None), P())
    return jax.shard_map(
        per_device,
        mesh=mesh,
        in_specs=placed,
        out_specs=(P("dp", "vocab", None), P("vocab", None), P()),
        check_vma=False,
    )
```

profile of v0, /device:TPU:1, one launch (start us, length us, event | category | flops | bytes accessed | tf_op | source)
XLA Modules:
  0.0 489.9 jit_solution(14090713662110557469)
XLA Ops:
  7.2 0.0 copy-start
  7.2 0.0 copy-start.1
  7.2 0.0 copy-start.2
  7.2 0.0 all-reduce.2.cloned.1.call-start
  7.2 0.9 copy-done
  8.2 3.5 fusion.3
  11.7 49.0 %psum.21 = f32[128,32]{0,1:T(8,128)S(1)} all-reduce(f32[128,32]{0,1:T(8,128)S(1)} %fusion.3), channel_id=1, replica_groups=mesh['dp'=16,'vocab'=32] {'dp'}, use_global_device_ids=true, to_apply=%region_0.0 | all-reduce | flops 4096 | bytes 32768 | tf_op jit(solution)/shard_map/psum | solution.py:20
  60.7 0.1 fusion.9
  60.9 118.7 %psum.22 = f32[32,32]{0,1:T(8,128)S(1)} all-reduce(f32[32,32]{0,1:T(8,128)S(1)} %fusion.9), channel_id=1, replica_groups=mesh['dp'=16,'vocab'=32] {'vocab'}, use_global_device_ids=true, to_apply=%region_1.0 | all-reduce | flops 1024 | bytes 8192 | tf_op jit(solution)/shard_map/psum | solution.py:21
  179.6 0.1 copy.7
  179.7 2.9 cholesky.16
  182.6 0.6 compare_reduce_fusion
  183.2 0.7 fusion.5
  183.9 2.4 custom-call.6
  186.3 0.2 fusion.6
  186.6 0.0 copy-done.1
  186.6 0.0 copy-done.2
  186.6 0.0 copy-start.4
  186.6 2.0 fusion.1
  188.6 0.0 all-reduce.2.cloned.1.call-update
  188.6 290.4 %all-reduce.2.cloned.1.call-done = f32[3584,32]{0,1:T(8,128)} async-done(((f32[3584,32]{0,1:T(8,128)}), f32[3584,32]{0,1:T(8,128)}) %all-reduce.2.cloned.1.call-update) | async-done | bytes 458768 | tf_op jit(solution)/shard_map/psum | solution.py:8
  479.0 1.0 broadcast_multiply_fusion
  480.0 0.0 copy-done.4
  480.1 0.0 copy-start.3
  480.1 2.9 fusion
  483.0 0.0 copy-done.3
  (2 shorter events, 0.0 us)
Async XLA Ops:
  7.2 1.0 copy-start
  7.2 179.4 %copy-start.1 = (f32[1,128,3584]{2,1,0:T(8,128)S(1)}, f32[1,128,3584]{2,1,0:T(8,128)}, u32[]{:S(2)}) copy-start(f32[1,128,3584]{2,1,0:T(8,128)} %param.4) | copy-start | bytes 5505028
  7.2 179.4 %copy-start.2 = (bf16[1,128,3584]{2,1,0:T(8,128)(2,1)S(1)}, bf16[1,128,3584]{2,1,0:T(8,128)(2,1)}, u32[]{:S(2)}) copy-start(bf16[1,128,3584]{2,1,0:T(8,128)(2,1)} %param.3) | copy-start | bytes 2752516
  7.2 471.8 %all-reduce.2.cloned.1.call-start = ((), (), s32[]{:S(2)}) async-start(), calls=%async_computation | async-start | bytes 917504 | tf_op jit(solution)/shard_map/psum | solution.py:8
  186.6 293.4 %copy-start.4 = (f32[128,32]{0,1:T(8,128)}, f32[128,32]{0,1:T(8,128)S(1)}, u32[]{:S(2)}) copy-start(f32[128,32]{0,1:T(8,128)S(1)} %fusion.6) | copy-start | bytes 49156
  480.1 3.0 copy-start.3
Sparse Core Ops, SparseCore 0:
  188.8 290.1 all-reduce.1
where the time goes:
time: 490 us
  waiting for transfers between devices  290 us (59%)
  blocking collectives  168 us (34%)
  between operations  14.1 us (3%)
  matrix products  8.82 us (2%)
  other arithmetic  7.74 us (2%)
    psum x1, waiting for transfers between devices, reduce_right(): return lax.psum(product, ('dp', 'vocab'))  290 us
    psum x1, blocking collectives, per_device(): gram = lax.psum(jnp.dot(p_sum.T, p_sum, precision=highest), 'vocab')  119 us
    psum x1, blocking collectives, per_device(): p_sum = lax.psum(p_local, 'dp')  49 us
  transfers between devices with their start and end apart: 1, of which 1 were waited for; matrix products, arithmetic and copies ran while one was open for 0% of the time, Pallas kernels for 0%

commit v1 on v0

v1 whole, which is shorter than its diff:
```python
import jax
import jax.numpy as jnp
from jax import lax
from jax.sharding import Mesh, PartitionSpec as P

HIGHEST = lax.Precision.HIGHEST
HIGH = lax.Precision.HIGH
DP = ("y", "core")
VOCAB = ("z", "x")


def gather_by_exchange(value, axes):
    members = lax.axis_size(axes)
    return lax.all_to_all(jnp.broadcast_to(value[None], (members,) + value.shape), axes, 0, 0)


def sum_by_exchange(value, axes):
    return jnp.sum(gather_by_exchange(value, axes), axis=0)


def per_device(grad, error, q_prev):
    rows, width = grad.shape[1:]
    rank = q_prev.shape[1]
    replicas = lax.axis_size(DP)
    half = width // 2
    core = lax.axis_index("core")
    merged = grad[0].astype(jnp.float32) + error[0]

    given = lax.dynamic_slice_in_dim(merged, (1 - core) * half, half, axis=1)
    taken = lax.ppermute(given, "core", [(0, 1), (1, 0)])

    p_local = lax.dot_general(q_prev, merged, (((0,), (1,)), ((), ())), precision=HIGHEST)
    p_sum = sum_by_exchange(p_local, DP)
    gram = lax.dot_general(p_sum, p_sum, (((1,), (1,)), ((), ())), precision=HIGHEST)

    chip_half = lax.dynamic_slice_in_dim(merged, core * half, half, axis=1) + taken
    right = jnp.dot(p_sum, chip_half, precision=HIGHEST)

    ny = lax.axis_size("y")
    pieces = right.reshape(rank // 8, 8, 2, half // 2).transpose(0, 2, 1, 3).reshape(ny, 8, half // 2)
    piece = jnp.sum(lax.all_to_all(pieces, "y", 0, 0), axis=0)

    packed_gram = gram.reshape(4, 8, rank).transpose(1, 0, 2).reshape(8, 4 * rank)
    packed = jnp.concatenate([piece, packed_gram], axis=1)
    packed = sum_by_exchange(packed, "x")
    packed = sum_by_exchange(packed, "z")
    piece, packed_gram = packed[:, : half // 2], packed[:, half // 2 :]
    gram = packed_gram.reshape(8, 4, rank).transpose(1, 0, 2).reshape(rank, rank)

    chol = jnp.linalg.cholesky(gram)
    inverse = lax.linalg.triangular_solve(chol, jnp.eye(rank, dtype=jnp.float32), left_side=True, lower=True)
    basis = jnp.dot(inverse, p_sum, precision=HIGHEST)

    own_half = gather_by_exchange(piece, "y")
    whole = lax.all_gather(own_half, "core")
    right = whole.reshape(2, rank // 8, 2, 8, half // 2).transpose(1, 3, 0, 2, 4).reshape(rank, width)
    q_new = jnp.dot(inverse / replicas, right, precision=HIGHEST)
    approx = lax.dot_general(basis, q_new, (((0,), (0,)), ((), ())), precision=HIGH)
    new_error = merged - approx
    return (new_error[None], basis.T, q_new.T)


def solution(mesh):
    fine = Mesh(mesh.devices.reshape(8, 2, 8, 4), DP + VOCAB)
    placed = (P(DP, VOCAB, None), P(DP, VOCAB, None), P())
    return jax.shard_map(
        per_device,
        mesh=fine,
        in_specs=placed,
        out_specs=(P(DP, VOCAB, None), P(VOCAB, None), P()),
        check_vma=False,
    )
```

time: 490 us -> 106 us (0.22)
  waiting for transfers between devices: 290 us -> 31.6 us
  blocking collectives: 168 us -> 32.6 us
  starting transfers between devices: 0.04 us -> 19 us
  between operations: 14.1 us -> 0.85 us
    psum x1 -> x0, waiting for transfers between devices: 290 us -> none  [reduce_right(): return lax.psum(product, ('dp', 'vocab'))]
    psum x2 -> x0, blocking collectives: 168 us -> none  [the longest x1 119 us: per_device(): gram = lax.psum(jnp.dot(p_sum.T, p_sum, precision=highest), 'vocab')]
    all_to_all x0 -> x3, waiting for transfers between devices: none -> 31.6 us  [the longest x2 20.3 us: gather_by_exchange(): lax.all_to_all(jnp.broadcast_to(value[None], (members,) + value.shape), a...]
    all_to_all x0 -> x2, blocking collectives: none -> 26.2 us  [gather_by_exchange(): lax.all_to_all(jnp.broadcast_to(value[None], (members,) + value.shape), a...]
    all_to_all x0 -> x3, starting transfers between devices: none -> 10.2 us  [the longest x2 6.83 us: gather_by_exchange(): lax.all_to_all(jnp.broadcast_to(value[None], (members,) + value.shape), a...]
    ppermute x0 -> x1, starting transfers between devices: none -> 8.79 us  [per_device(): taken = lax.ppermute(given, 'core', [(0, 1), (1, 0)])]
    all_gather x0 -> x1, blocking collectives: none -> 6.45 us  [per_device(): whole = lax.all_gather(own_half, 'core')]
  transfers between devices with their start and end apart: 1 -> 4, of which waited for: 1 -> 3; matrix products, arithmetic and copies ran while one was open for 0% -> 3% of each run, Pallas kernels for 0% -> 0%
where the time goes in v1:
time: 106 us
  blocking collectives  32.6 us (31%)
  waiting for transfers between devices  31.6 us (30%)
  starting transfers between devices  19 us (18%)
  other arithmetic  11 us (10%)
  matrix products  6.65 us (6%)
  local copies, waits for them, and re-layouts  3.91 us (4%)
    all_to_all x2, blocking collectives, gather_by_exchange(): lax.all_to_all(jnp.broadcast_to(value[None], (members,) + value.shape), a...  26.2 us
    all_to_all x2, waiting for transfers between devices, gather_by_exchange(): lax.all_to_all(jnp.broadcast_to(value[None], (members,) + value.shape), a...  20.3 us
    all_to_all x1, waiting for transfers between devices, per_device(): piece = jnp.sum(lax.all_to_all(pieces, 'y', 0, 0), axis=0)  11.3 us
    ppermute x1, starting transfers between devices, per_device(): taken = lax.ppermute(given, 'core', [(0, 1), (1, 0)])  8.79 us
    all_to_all x2, starting transfers between devices, gather_by_exchange(): lax.all_to_all(jnp.broadcast_to(value[None], (members,) + value.shape), a...  6.83 us
    all_gather x1, blocking collectives, per_device(): whole = lax.all_gather(own_half, 'core')  6.45 us
    another operation x3, other arithmetic, per_device(): chol = jnp.linalg.cholesky(gram)  3.6 us
    all_to_all x1, starting transfers between devices, per_device(): piece = jnp.sum(lax.all_to_all(pieces, 'y', 0, 0), axis=0)  3.4 us
  transfers between devices with their start and end apart: 4, of which 3 were waited for; matrix products, arithmetic and copies ran while one was open for 3% of the time, Pallas kernels for 0%

profile of v1, /device:TPU:1, one launch (start us, length us, event | category | flops | bytes accessed | tf_op | source)
XLA Modules:
  0.0 105.6 jit_solution(109616970677171542)
XLA Ops:
  0.6 0.0 copy-start
  0.7 2.0 %convert_add_fusion = f32[1,128,3584]{2,1,0:T(8,128)S(1)} fusion(f32[1,128,3584]{2,1,0:T(8,128)} %param.4, bf16[1,128,3584]{2,1,0:T(8,128)(2,1)} %param.3), kind=kLoop, calls=%fused_computation.4 | loop fusion | flops 917504 | bytes 4587520 | tf_op jit(solution)/shard_map/add | solution.py:27
  2.6 0.1 dynamic-slice_bitcast_fusion
  2.7 8.8 %collective-permute-start = (f32[128,1792]{1,0:T(8,128)S(1)}, f32[128,1792]{1,0:T(8,128)}, u32[]{:S(2)}, u32[]{:S(2)}) collective-permute-start(f32[128,1792]{1,0:T(8,128)S(1)} %dynamic-slice_bitcast_fusion), channel_id=1, source_target_pairs={{0,32},{32,0},{1,33},{33,1},{2,34},{34,2},{3,35},{35,3},{4,36},{36... | collective-permute-start | bytes 2752520 | tf_op jit(solution)/shard_map/ppermute | solution.py:30
  11.5 0.0 copy-done
  11.5 1.8 %fusion.3 = f32[32,128]{1,0:T(8,128)S(1)} fusion(f32[3584,32]{0,1:T(8,128)S(1)} %copy-done, f32[1,128,3584]{2,1,0:T(8,128)S(1)} %convert_add_fusion), kind=kOutput, calls=%fused_computation.6 | convolution fusion | flops 176160768 | bytes 2310144 | tf_op jit(solution)/shard_map/dot_general | solution.py:32
  13.3 0.7 broadcast_in_dim.11
  14.0 3.4 %all-to-all-start = ((f32[16,32,128]{2,1,0:T(8,128)}), f32[16,32,128]{2,1,0:T(8,128)S(1)}, u32[]{:S(2)}, u32[]{:S(2)}) async-start(f32[16,32,128]{2,1,0:T(8,128)} %broadcast_in_dim.11), calls=%async_computation | async-start | bytes 524288 | tf_op jit(solution)/shard_map/all_to_all | solution.py:14
  17.5 11.8 %all-to-all-done = f32[16,32,128]{2,1,0:T(8,128)S(1)} async-done(((f32[16,32,128]{2,1,0:T(8,128)}), f32[16,32,128]{2,1,0:T(8,128)S(1)}, u32[]{:S(2)}, u32[]{:S(2)}) %all-to-all-start) | async-done | bytes 262176 | tf_op jit(solution)/shard_map/all_to_all | solution.py:14
  29.3 0.0 collective-permute-done
  29.3 2.2 %fusion.6 = f32[1792,128]{0,1:T(8,128)} fusion(f32[128,1792]{1,0:T(8,128)} %collective-permute-done, f32[1,128,3584]{2,1,0:T(8,128)S(1)} %convert_add_fusion, s32[]{:T(128)S(6)} %select_n.10), kind=kLoop, calls=%fused_computation.8 | loop fusion | flops 229376 | bytes 2752516 | tf_op jit(solution)/shard_map/dot_general | solution.py:37
  31.5 1.5 %copy.27 = f32[1792,128]{1,0:T(8,128)S(1)} copy(f32[1792,128]{0,1:T(8,128)} %fusion.6) | data formatting | bytes 1835008 | tf_op jit(solution)/shard_map/dot_general | solution.py:37
  33.0 1.7 %fusion.8 = f32[4,8,2,896]{3,1,2,0:T(8,128)} fusion(f32[2,896,128,1]{2,1,0,3:T(8,128)S(1)} %bitcast.65, f32[32,128]{1,0:T(8,128)S(1)} %reduce_sum.36), kind=kOutput, calls=%fused_computation.13 | convolution fusion | flops 88080384 | bytes 1163264 | tf_op jit(solution)/shard_map/dot_general | solution.py:37
  34.7 3.4 %all-to-all-start.1 = ((f32[8,8,896]{2,1,0:T(8,128)}), f32[8,8,896]{2,1,0:T(8,128)S(1)}, u32[]{:S(2)}, u32[]{:S(2)}) async-start(f32[8,8,896]{2,1,0:T(8,128)} %bitcast.11), calls=%async_computation.1 | async-start | bytes 458752 | tf_op jit(solution)/shard_map/all_to_all | solution.py:41
  38.1 0.1 convolution_bitcast_fusion
  38.3 0.1 reshape.47
  38.4 11.3 %all-to-all-done.1 = f32[8,8,896]{2,1,0:T(8,128)S(1)} async-done(((f32[8,8,896]{2,1,0:T(8,128)}), f32[8,8,896]{2,1,0:T(8,128)S(1)}, u32[]{:S(2)}, u32[]{:S(2)}) %all-to-all-start.1) | async-done | bytes 229408 | tf_op jit(solution)/shard_map/all_to_all | solution.py:41
  49.7 7.2 %all_to_all.25 = f32[4,8,1024]{2,1,0:T(8,128)S(1)} all-to-all(f32[4,8,1024]{2,1,0:T(8,128)S(1)} %broadcast_in_dim.12), channel_id=1, replica_groups=mesh['y'=8,'core'=2,'z'=8,'x'=4] {'x'}, dimensions={0} | all-to-all | bytes 262144 | tf_op jit(solution)/shard_map/all_to_all | solution.py:14
  56.9 19.0 %all_to_all.26 = f32[8,8,1024]{2,1,0:T(8,128)S(1)} all-to-all(f32[8,8,1024]{2,1,0:T(8,128)S(1)} %broadcast_in_dim.14), channel_id=1, replica_groups=mesh['y'=8,'core'=2,'z'=8,'x'=4] {'z'}, dimensions={0} | all-to-all | bytes 524288 | tf_op jit(solution)/shard_map/all_to_all | solution.py:14
  76.0 0.1 reshape.48
  76.0 0.1 copy.24
  76.1 2.9 %cholesky.17 = f32[32,32]{1,0:T(8,128)S(1)} custom-call(f32[32,32]{1,0:T(8,128)S(1)} %fusion.12), custom_call_target="Cholesky" | custom-call | tf_op jit(solution)/shard_map/jit(cholesky)/cholesky | solution.py:50
  79.1 0.6 compare_reduce_fusion
  79.7 0.7 fusion.7
  80.4 2.4 %custom-call.6 = f32[1,32,32]{1,2,0:T(8,128)S(1)} custom-call(f32[1,32,32]{2,1,0:T(8,128)S(1)} %fusion.7), custom_call_target="InvertDiagBlocksLowerTriangular" | custom-call | tf_op jit(solution)/shard_map/triangular_solve | solution.py:51
  82.8 0.7 broadcast_in_dim.15
  83.5 3.4 %all-to-all-start.4 = ((f32[8,8,896]{2,1,0:T(8,128)}), f32[8,8,896]{2,1,0:T(8,128)S(1)}, u32[]{:S(2)}, u32[]{:S(2)}) async-start(f32[8,8,896]{2,1,0:T(8,128)} %broadcast_in_dim.15), calls=%async_computation.4 | async-start | bytes 458752 | tf_op jit(solution)/shard_map/all_to_all | solution.py:14
  87.0 0.2 fusion.10
  87.1 0.1 fusion.19
  87.3 0.0 copy-start.2
  87.3 8.6 %all-to-all-done.4 = f32[8,8,896]{2,1,0:T(8,128)S(1)} async-done(((f32[8,8,896]{2,1,0:T(8,128)}), f32[8,8,896]{2,1,0:T(8,128)S(1)}, u32[]{:S(2)}, u32[]{:S(2)}) %all-to-all-start.4) | async-done | bytes 229408 | tf_op jit(solution)/shard_map/all_to_all | solution.py:14
  95.9 6.4 %all-gather = f32[16,8,896]{2,1,0:T(8,128)S(1)} all-gather(f32[8,8,896]{2,1,0:T(8,128)S(1)} %all-to-all-done.4), channel_id=2, replica_groups=mesh['y'=8,'core'=2,'z'=8,'x'=4] {'core'}, dimensions={0}, use_global_device_ids=true | all-gather | bytes 688128 | tf_op jit(solution)/shard_map/all_gather | solution.py:55
  102.3 0.2 copy.25
  102.6 0.4 reshape.51
  103.0 0.5 fusion.15
  103.5 0.0 copy-start.1
  103.5 2.1 %fusion = f32[1,128,3584]{2,1,0:T(8,128)} fusion(f32[32,128]{1,0:T(8,128)S(1)} %fusion.19, f32[32,3584]{1,0:T(8,128)S(1)} %fusion.15, f32[1,128,3584]{2,1,0:T(8,128)S(1)} %convert_add_fusion), kind=kOutput, calls=%fused_computation.1 | convolution fusion | flops 88539136 | bytes 4145152 | tf_op jit(solution)/shard_map/dot_general | solution.py:58
  105.6 0.0 copy-done.2
  105.6 0.0 copy-done.1
  (13 shorter events, 0.2 us)
Async XLA Ops:
  0.6 10.9 %copy-start = (f32[3584,32]{0,1:T(8,128)S(1)}, f32[3584,32]{0,1:T(8,128)}, u32[]{:S(2)}) copy-start(f32[3584,32]{0,1:T(8,128)} %param.5) | copy-start | bytes 1376260
  2.7 26.6 %collective-permute-start = (f32[128,1792]{1,0:T(8,128)S(1)}, f32[128,1792]{1,0:T(8,128)}, u32[]{:S(2)}, u32[]{:S(2)}) collective-permute-start(f32[128,1792]{1,0:T(8,128)S(1)} %dynamic-slice_bitcast_fusion), channel_id=1, source_target_pairs={{0,32},{32,0},{1,33},{33,1},{2,34},{34,2},{3,35},{35,3},{4,36},{36... | collective-permute-start | bytes 2752520 | tf_op jit(solution)/shard_map/ppermute | solution.py:30
  14.0 15.2 %all-to-all-start = ((f32[16,32,128]{2,1,0:T(8,128)}), f32[16,32,128]{2,1,0:T(8,128)S(1)}, u32[]{:S(2)}, u32[]{:S(2)}) async-start(f32[16,32,128]{2,1,0:T(8,128)} %broadcast_in_dim.11), calls=%async_computation | async-start | bytes 524288 | tf_op jit(solution)/shard_map/all_to_all | solution.py:14
  34.7 14.9 %all-to-all-start.1 = ((f32[8,8,896]{2,1,0:T(8,128)}), f32[8,8,896]{2,1,0:T(8,128)S(1)}, u32[]{:S(2)}, u32[]{:S(2)}) async-start(f32[8,8,896]{2,1,0:T(8,128)} %bitcast.11), calls=%async_computation.1 | async-start | bytes 458752 | tf_op jit(solution)/shard_map/all_to_all | solution.py:41
  83.5 12.3 %all-to-all-start.4 = ((f32[8,8,896]{2,1,0:T(8,128)}), f32[8,8,896]{2,1,0:T(8,128)S(1)}, u32[]{:S(2)}, u32[]{:S(2)}) async-start(f32[8,8,896]{2,1,0:T(8,128)} %broadcast_in_dim.15), calls=%async_computation.4 | async-start | bytes 458752 | tf_op jit(solution)/shard_map/all_to_all | solution.py:14
  87.3 18.3 %copy-start.2 = (f32[32,128]{1,0:T(8,128)}, f32[32,128]{1,0:T(8,128)S(1)}, u32[]{:S(2)}) copy-start(f32[32,128]{1,0:T(8,128)S(1)} %fusion.19) | copy-start | bytes 49156
  103.5 2.2 %copy-start.1 = (f32[32,3584]{1,0:T(8,128)}, f32[32,3584]{1,0:T(8,128)S(1)}, u32[]{:S(2)}) copy-start(f32[32,3584]{1,0:T(8,128)S(1)} %fusion.15) | copy-start | bytes 1376260

commit v2 on v0

v2 whole, which is shorter than its diff:
```python
import functools

import jax
import jax.numpy as jnp
from jax import lax
from jax.experimental import pallas as pl
from jax.experimental.pallas import tpu as pltpu
from jax.sharding import Mesh, PartitionSpec as P

F32, BF16 = jnp.float32, jnp.bfloat16
HIGHEST = lax.Precision.HIGHEST
DP = ("y", "core")
VOCAB = ("z", "x")
NY, NX, NZ = 8, 4, 8
RANK, ROWS, WIDTH = 32, 128, 3584
HALF = WIDTH // 2
LANES = 128
TILES = HALF // LANES
PIECE = TILES + 2
VMEM_LIMIT = 48 * 1024 * 1024

NT = (((1,), (1,)), ((), ()))
NN = (((1,), (0,)), ((), ()))


def split3(value):
    high = value.astype(BF16)
    rest = value - high.astype(F32)
    middle = rest.astype(BF16)
    low = (rest - middle.astype(F32)).astype(BF16)
    return high, middle, low


def dot(a, b, dims=NN):
    return lax.dot_general(a, b, dims, preferred_element_type=F32)


def stack_left(value):
    h, m, l = split3(value)
    return jnp.concatenate([h, h, m, m, h, l], axis=1)


def stack_right(value):
    h, m, l = split3(value)
    return jnp.concatenate([h, m, h, m, l, h], axis=0)


def kernel_call(body, out_shape, **options):
    return pl.pallas_call(
        body,
        out_shape=out_shape,
        compiler_params=pltpu.CompilerParams(vmem_limit_bytes=VMEM_LIMIT),
        **options,
    )


def shape(*dims):
    return jax.ShapeDtypeStruct(dims, F32)


def left_body(core_ref, grad_ref, error_ref, q_ref, p_ref, given_ref):
    step = pl.program_id(0)
    merged = grad_ref[...].astype(F32) + error_ref[...]

    @pl.when(step == 0)
    def _():
        given_ref[...] = merged

    left = jnp.concatenate(split3(merged), axis=0)
    right = jnp.concatenate(split3(q_ref[...]), axis=0)
    product = dot(left, right, NT)
    total = product[:ROWS]
    for part in range(1, 3):
        total += product[part * ROWS : (part + 1) * ROWS]
    total = total[:, :RANK] + (total[:, RANK : 2 * RANK] + total[:, 2 * RANK :])

    @pl.when(step == 0)
    def _():
        p_ref[...] = total.T

    @pl.when(step == 1)
    def _():
        p_ref[...] += total.T


def left_product(core, grad, error, q_rows):
    columns = lambda j, core: (0, (1 - core[0] + j) % 2)
    return pl.pallas_call(
        left_body,
        out_shape=(shape(RANK, ROWS), shape(ROWS, HALF)),
        grid_spec=pltpu.PrefetchScalarGridSpec(
            num_scalar_prefetch=1,
            grid=(2,),
            in_specs=[
                pl.BlockSpec((ROWS, HALF), columns),
                pl.BlockSpec((ROWS, HALF), columns),
                pl.BlockSpec((RANK, HALF), columns),
            ],
            out_specs=[
                pl.BlockSpec((RANK, ROWS), lambda j, core: (0, 0)),
                pl.BlockSpec((ROWS, HALF), lambda j, core: (0, 0)),
            ],
        ),
        compiler_params=pltpu.CompilerParams(vmem_limit_bytes=VMEM_LIMIT),
    )(core, grad, error, q_rows)


def right_body(place_ref, parts_ref, grad_ref, error_ref, taken_ref, pieces_ref, p_ref):
    p_sum = jnp.sum(parts_ref[...], axis=0)
    p_ref[...] = p_sum
    columns = grad_ref[...].astype(F32) + error_ref[...] + taken_ref[...]
    p_parts = jnp.concatenate(split3(p_sum), axis=0)
    h, m, l = split3(columns)
    with_h = dot(p_parts, h)
    with_m = dot(p_parts[: 2 * RANK], m)
    with_l = dot(p_parts[:RANK], l)
    small = with_h[2 * RANK :] + with_m[RANK:] + with_l
    product = with_h[:RANK] + (with_h[RANK : 2 * RANK] + with_m[:RANK] + small)
    for tile in range(TILES):
        pieces_ref[:, tile, :] = product[:, tile * LANES : (tile + 1) * LANES]
    gram = lax.dot_general(p_sum, p_sum, NT, precision=HIGHEST, preferred_element_type=F32)
    packed = jnp.concatenate([gram[8 * a : 8 * a + 8] for a in range(4)], axis=1)
    mine = lax.broadcasted_iota(jnp.int32, (8, LANES), 0) == place_ref[1]
    row = jnp.sum(jnp.where(mine, packed, 0.0), axis=0, keepdims=True)
    pieces_ref[:, TILES, :] = jnp.broadcast_to(row, (RANK, LANES))
    pieces_ref[:, TILES + 1, :] = jnp.zeros((RANK, LANES), F32)


def right_product(place, parts, grad, error, taken):
    columns = lambda j, place: (0, place[0])
    whole = lambda j, place: (0, 0)
    return pl.pallas_call(
        right_body,
        out_shape=(shape(RANK, PIECE, LANES), shape(RANK, ROWS)),
        grid_spec=pltpu.PrefetchScalarGridSpec(
            num_scalar_prefetch=1,
            grid=(1,),
            in_specs=[
                pl.BlockSpec((NY, RANK, ROWS), lambda j, place: (0, 0, 0)),
                pl.BlockSpec((ROWS, HALF), columns),
                pl.BlockSpec((ROWS, HALF), columns),
                pl.BlockSpec((ROWS, HALF), whole),
            ],
            out_specs=[
                pl.BlockSpec((RANK, PIECE, LANES), lambda j, place: (0, 0, 0)),
                pl.BlockSpec((RANK, ROWS), whole),
            ],
        ),
        compiler_params=pltpu.CompilerParams(vmem_limit_bytes=VMEM_LIMIT),
    )(place, parts, grad, error, taken)


def plane_body(parts_ref, out_ref):
    rows = parts_ref[0]
    for member in range(1, NY * NX):
        rows += parts_ref[member]
    gram = [sum(parts_ref[y * NX + x, TILES : TILES + 1, :] for x in range(NX)) for y in range(NY)]
    both = jnp.concatenate([rows] + gram, axis=0)
    for z in range(NZ):
        out_ref[z] = both


def line_body(parts_ref, out_ref):
    rows = parts_ref[0, :PIECE, :]
    for z in range(1, NZ):
        rows += parts_ref[z, :PIECE, :]
    for member in range(NY * NX):
        out_ref[member] = rows


def factor_body(replicas, parts_ref, p_ref, basis_ref, basis_stack_ref, inverse_stack_ref):
    packed = parts_ref[0, PIECE:, :]
    for z in range(1, NZ):
        packed += parts_ref[z, PIECE:, :]
    gram = jnp.concatenate([packed[:, RANK * a : RANK * (a + 1)] for a in range(4)], axis=0)
    row = lax.broadcasted_iota(jnp.int32, (RANK, RANK), 0)
    column = lax.broadcasted_iota(jnp.int32, (RANK, RANK), 1)
    unit = jnp.where(row == column, 1.0, 0.0).astype(F32)
    work = jnp.concatenate([gram, unit], axis=1)
    below = lax.broadcasted_iota(jnp.int32, (RANK, 1), 0)
    inverse = []
    for j in range(RANK):
        pivot_row = work[j : j + 1, :]
        pivot = pivot_row[:, j : j + 1]
        inverse.append(pivot_row[:, RANK:] / jnp.sqrt(pivot))
        if j < RANK - 1:
            factor = jnp.where(below > j, work[:, j : j + 1] / pivot, 0.0)
            work = work - factor * pivot_row
    inverse = jnp.concatenate(inverse, axis=0)
    basis = lax.dot_general(inverse, p_ref[...], NN, precision=HIGHEST, preferred_element_type=F32)
    basis_ref[...] = basis
    basis_stack_ref[...] = stack_left(basis.T)
    inverse_stack_ref[...] = stack_left(inverse * (1.0 / replicas))


def final_body(parts_ref, inverse_ref, basis_ref, grad_ref, error_ref, out_ref, q_ref):
    right = jnp.concatenate([parts_ref[0, :, tile, :] for tile in range(TILES)], axis=1)
    q_new = dot(inverse_ref[...], stack_right(right))
    q_ref[...] = q_new
    approx = dot(basis_ref[...], stack_right(q_new))
    out_ref[...] = (grad_ref[...].astype(F32) + error_ref[...]) - approx


def final(parts, inverse_stack, basis_stack, grad, error):
    columns = lambda j: (0, j)
    whole = lambda j: (0, 0)
    return kernel_call(
        final_body,
        (shape(ROWS, WIDTH), shape(RANK, WIDTH)),
        grid=(2,),
        in_specs=[
            pl.BlockSpec((1, RANK, PIECE, LANES), lambda j: (j, 0, 0, 0)),
            pl.BlockSpec((RANK, 6 * RANK), whole),
            pl.BlockSpec((ROWS, 6 * RANK), whole),
            pl.BlockSpec((ROWS, HALF), columns),
            pl.BlockSpec((ROWS, HALF), columns),
        ],
        out_specs=[pl.BlockSpec((ROWS, HALF), columns), pl.BlockSpec((RANK, HALF), columns)],
    )(parts, inverse_stack, basis_stack, grad, error)


def per_device(grad, error, q_prev):
    grad, error = grad[0], error[0]
    replicas = lax.axis_size(DP)
    place = jnp.stack([lax.axis_index("core"), lax.axis_index("y")]).astype(jnp.int32)

    p_local, given = left_product(place, grad, error, q_prev.T)
    taken = lax.ppermute(given, "core", [(0, 1), (1, 0)])
    p_chip = jnp.sum(lax.all_gather(p_local, "core"), axis=0)
    p_parts = lax.all_to_all(jnp.broadcast_to(p_chip[None], (NY, RANK, ROWS)), "y", 0, 0)

    pieces, p_sum = right_product(place, p_parts, grad, error, taken)
    pieces = lax.all_to_all(pieces, ("y", "x"), 0, 0)
    lines = kernel_call(plane_body, shape(NZ, PIECE + 8, LANES))(pieces)
    lines = lax.all_to_all(lines, "z", 0, 0)
    own = kernel_call(line_body, shape(NY * NX, PIECE, LANES))(lines)
    own = lax.all_to_all(own, ("y", "x"), 0, 0)
    basis, basis_stack, inverse_stack = kernel_call(
        functools.partial(factor_body, replicas),
        (
            shape(RANK, ROWS),
            jax.ShapeDtypeStruct((ROWS, 6 * RANK), BF16),
            jax.ShapeDtypeStruct((RANK, 6 * RANK), BF16),
        ),
    )(lines, p_sum)
    whole = lax.all_gather(own, "core")
    new_error, q_new = final(whole, inverse_stack, basis_stack, grad, error)
    return (new_error[None], basis.T, q_new.T)


def solution(mesh):
    fine = Mesh(mesh.devices.reshape(NY, 2, NZ, NX), DP + VOCAB)
    placed = (P(DP, VOCAB, None), P(DP, VOCAB, None), P())
    return jax.shard_map(
        per_device,
        mesh=fine,
        in_specs=placed,
        out_specs=(P(DP, VOCAB, None), P(VOCAB, None), P()),
        check_vma=False,
    )
```

time: 490 us -> 88.6 us (0.18)
  waiting for transfers between devices: 290 us -> 6.94 us
  blocking collectives: 168 us -> 50.7 us
  starting transfers between devices: 0.04 us -> 13.9 us
  between operations: 14.1 us -> 0.68 us
  Pallas kernels: 0 us -> 12.1 us
  matrix products: 8.82 us -> 0 us
  other arithmetic: 7.74 us -> 0.08 us
    psum x1 -> x0, waiting for transfers between devices: 290 us -> none  [reduce_right(): return lax.psum(product, ('dp', 'vocab'))]
    psum x2 -> x0, blocking collectives: 168 us -> none  [the longest x1 119 us: per_device(): gram = lax.psum(jnp.dot(p_sum.T, p_sum, precision=highest), 'vocab')]
    all_to_all x0 -> x3, blocking collectives: none -> 42.2 us  [the longest x1 17.4 us: per_device(): lines = lax.all_to_all(lines, 'z', 0, 0)]
    pallas_call x0 -> x6, Pallas kernels: none -> 12.1 us  [the longest x1 3.5 us: left_product(): pl.pallas_call(left_body, out_shape=(shape(RANK, ROWS), shape(ROWS, HALF)...]
    ppermute x0 -> x1, starting transfers between devices: none -> 8.78 us  [per_device(): taken = lax.ppermute(given, 'core', [(0, 1), (1, 0)])]
    dot_general x4 -> x0, matrix products: 8.59 us -> none  [the longest x1 3.51 us: per_device(): p_local = jnp.dot(merged, q_prev, precision=highest)]
    all_gather x0 -> x2, blocking collectives: none -> 8.46 us  [the longest x1 6.35 us: per_device(): whole = lax.all_gather(own, 'core')]
    all_to_all x0 -> x1, waiting for transfers between devices: none -> 6.94 us  [per_device(): own = lax.all_to_all(own, ('y', 'x'), 0, 0)]
  transfers between devices with their start and end apart: 1 -> 2, of which waited for: 1 -> 1; matrix products, arithmetic and copies ran while one was open for 0% -> 0% of each run, Pallas kernels for 0% -> 4%
where the time goes in v2:
time: 88.6 us; the launch traced here: 88.1 us
  blocking collectives  50.7 us (57%)
  starting transfers between devices  13.9 us (16%)
  Pallas kernels  12.1 us (14%)
  waiting for transfers between devices  6.94 us (8%)
  local copies, waits for them, and re-layouts  3.72 us (4%)
    all_to_all x1, blocking collectives, per_device(): lines = lax.all_to_all(lines, 'z', 0, 0)  17.4 us
    all_to_all x1, blocking collectives, per_device(): pieces = lax.all_to_all(pieces, ('y', 'x'), 0, 0)  14 us
    all_to_all x1, blocking collectives, per_device(): lax.all_to_all(jnp.broadcast_to(p_chip[None], (NY, RANK, ROWS)), 'y', 0, 0)  10.8 us
    ppermute x1, starting transfers between devices, per_device(): taken = lax.ppermute(given, 'core', [(0, 1), (1, 0)])  8.78 us
    all_to_all x1, waiting for transfers between devices, per_device(): own = lax.all_to_all(own, ('y', 'x'), 0, 0)  6.94 us
    all_gather x1, blocking collectives, per_device(): whole = lax.all_gather(own, 'core')  6.35 us
    all_to_all x1, starting transfers between devices, per_device(): own = lax.all_to_all(own, ('y', 'x'), 0, 0)  5.09 us
    unnamed x10, local copies, waits for them, and re-layouts  3.7 us
  transfers between devices with their start and end apart: 2, of which 1 were waited for; matrix products, arithmetic and copies ran while one was open for 0% of the time, Pallas kernels for 4%

profile of v2, /device:TPU:1, one launch (start us, length us, event | category | flops | bytes accessed | tf_op | source)
XLA Modules:
  0.0 88.1 jit_solution(17430098252501151612)
XLA Ops:
  0.6 0.1 pad_add_fusion.core_ref.place_ref
  0.7 0.0 copy-start
  0.7 1.5 %copy-done = f32[1,128,3584]{2,1,0:T(8,128)S(1)} copy-done((f32[1,128,3584]{2,1,0:T(8,128)S(1)}, f32[1,128,3584]{2,1,0:T(8,128)}, u32[]{:S(2)}) %copy-start) | copy-done | bytes 1835032
  2.2 0.0 copy-start.2
  2.2 1.2 %copy-done.2 = bf16[1,128,3584]{2,1,0:T(8,128)(2,1)S(1)} copy-done((bf16[1,128,3584]{2,1,0:T(8,128)(2,1)S(1)}, bf16[1,128,3584]{2,1,0:T(8,128)(2,1)}, u32[]{:S(2)}) %copy-start.2) | copy-done | bytes 917528
  3.4 0.0 copy-start.4
  3.4 1.0 %copy-done.4 = f32[3584,32]{0,1:T(8,128)S(1)} copy-done((f32[3584,32]{0,1:T(8,128)S(1)}, f32[3584,32]{0,1:T(8,128)}, u32[]{:S(2)}) %copy-start.4) | copy-done | bytes 458776
  4.4 0.0 copy-start.1
  4.4 0.0 copy-start.3
  4.4 3.5 %shard_map.58 = (f32[32,128]{1,0:T(8,128)S(1)}, f32[128,1792]{1,0:T(8,128)}) custom-call(s32[2]{0:T(128)S(1)} %pad_add_fusion.core_ref.place_ref, bf16[128,3584]{1,0:T(8,128)(2,1)S(1)} %bitcast.13, f32[128,3584]{1,0:T(8,128)S(1)} %bitcast.10, f32[32,3584]{1,0:T(8,128)S(1)} %bitcast.17), custom_call_target="tpu_custom_call" | custom-call | tf_op jit(solution)/shard_map/pallas_call | solution.py:88
  7.9 8.8 %collective-permute-start = (f32[128,1792]{1,0:T(8,128)}, f32[128,1792]{1,0:T(8,128)}, u32[]{:S(2)}, u32[]{:S(2)}) collective-permute-start(f32[128,1792]{1,0:T(8,128)} %get-tuple-element.13), channel_id=1, source_target_pairs={{0,32},{32,0},{1,33},{33,1},{2,34},{34,2},{3,35},{35,3},{4,36},{36... | collective-permute-start | bytes 2752520 | tf_op jit(solution)/shard_map/ppermute | solution.py:228
  16.7 2.1 %all-gather = f32[64,128]{1,0:T(8,128)S(1)} all-gather(f32[32,128]{1,0:T(8,128)S(1)} %get-tuple-element.12), channel_id=2, replica_groups=mesh['y'=8,'core'=2,'z'=8,'x'=4] {'core'}, dimensions={0}, use_global_device_ids=true | all-gather | bytes 49152 | tf_op jit(solution)/shard_map/all_gather | solution.py:229
  18.8 10.8 %all_to_all.20.parts_ref = f32[8,32,128]{2,1,0:T(8,128)S(1)} all-to-all(f32[8,32,128]{2,1,0:T(8,128)S(1)} %broadcast_in_dim.4), channel_id=1, replica_groups=mesh['y'=8,'core'=2,'z'=8,'x'=4] {'y'}, dimensions={0} | all-to-all | bytes 262144 | tf_op jit(solution)/shard_map/all_to_all | solution.py:230
  29.6 0.0 collective-permute-done.taken_ref
  29.6 0.0 copy-done.1
  29.6 0.0 copy-done.3
  29.6 2.3 %shard_map.59 = (f32[32,16,128]{2,1,0:T(8,128)S(1)}, f32[32,128]{1,0:T(8,128)S(1)}) custom-call(s32[2]{0:T(128)S(1)} %pad_add_fusion.core_ref.place_ref, f32[8,32,128]{2,1,0:T(8,128)S(1)} %all_to_all.20.parts_ref, bf16[128,3584]{1,0:T(8,128)(2,1)S(1)} %bitcast.14, f32[128,3584]{1,0:T(8,128)S(1)} %bitcast.11, f32[128,1792]{1,0:T(8,128)} %collective-permute-done.taken_ref), custom_call_target="tpu_custom_call" | custom-call | tf_op jit(solution)/shard_map/pallas_call | solution.py:132
  31.9 14.0 %all_to_all.21.parts_ref = f32[32,16,128]{2,1,0:T(8,128)S(1)} all-to-all(f32[32,16,128]{2,1,0:T(8,128)S(1)} %get-tuple-element.14), channel_id=1, replica_groups=mesh['y'=8,'core'=2,'z'=8,'x'=4] {'y','x'}, dimensions={0} | all-to-all | bytes 524288 | tf_op jit(solution)/shard_map/all_to_all | solution.py:233
  46.0 17.4 %all_to_all.22.parts_ref = f32[8,24,128]{2,1,0:T(8,128)S(1)} all-to-all(f32[8,24,128]{2,1,0:T(8,128)S(1)} %shard_map.60), channel_id=1, replica_groups=mesh['y'=8,'core'=2,'z'=8,'x'=4] {'z'}, dimensions={0} | all-to-all | bytes 196608 | tf_op jit(solution)/shard_map/all_to_all | solution.py:235
  63.4 0.7 shard_map.61
  64.1 5.1 %all-to-all-start.3 = ((f32[32,16,128]{2,1,0:T(8,128)}), f32[32,16,128]{2,1,0:T(8,128)S(1)}, u32[]{:S(2)}, u32[]{:S(2)}) async-start(f32[32,16,128]{2,1,0:T(8,128)} %shard_map.61), calls=%async_computation.3 | async-start | bytes 524288 | tf_op jit(solution)/shard_map/all_to_all | solution.py:237
  69.2 3.5 %shard_map.62 = (f32[32,128]{1,0:T(8,128)}, bf16[128,192]{1,0:T(8,128)(2,1)S(1)}, bf16[32,192]{1,0:T(8,128)(2,1)S(1)}) custom-call(f32[8,24,128]{2,1,0:T(8,128)S(1)} %all_to_all.22.parts_ref, f32[32,128]{1,0:T(8,128)S(1)} %get-tuple-element.15.p_ref), custom_call_target="tpu_custom_call" | custom-call | tf_op jit(solution)/shard_map/pallas_call | solution.py:238
  72.7 6.9 %all-to-all-done.3 = f32[32,16,128]{2,1,0:T(8,128)S(1)} async-done(((f32[32,16,128]{2,1,0:T(8,128)}), f32[32,16,128]{2,1,0:T(8,128)S(1)}, u32[]{:S(2)}, u32[]{:S(2)}) %all-to-all-start.3) | async-done | bytes 262176 | tf_op jit(solution)/shard_map/all_to_all | solution.py:237
  79.6 6.4 %all-gather.1 = f32[64,16,128]{2,1,0:T(8,128)S(1)} all-gather(f32[32,16,128]{2,1,0:T(8,128)S(1)} %all-to-all-done.3), channel_id=3, replica_groups=mesh['y'=8,'core'=2,'z'=8,'x'=4] {'core'}, dimensions={0}, use_global_device_ids=true | all-gather | bytes 786432 | tf_op jit(solution)/shard_map/all_gather | solution.py:246
  85.9 2.2 %shard_map.63 = (f32[128,3584]{1,0:T(8,128)}, f32[32,3584]{1,0:T(8,128)}) custom-call(f32[2,32,16,128]{3,2,1,0:T(8,128)S(1)} %bitcast.16, bf16[32,192]{1,0:T(8,128)(2,1)S(1)} %get-tuple-element.16.inverse_ref, bf16[128,192]{1,0:T(8,128)(2,1)S(1)} %get-tuple-element.17.basis_ref, bf16[128,3584]{1,0:T(8,128)(2,1)S(1)} %bitcast.15, f32[128,3584]{1,0:T(8,128)S(1)} %bitcast.12), custom_call_target="tpu_custom_call" | custom-call | tf_op jit(solution)/shard_map/pallas_call | solution.py:207
  (3 shorter events, 0.1 us)
Async XLA Ops:
  0.7 1.5 %copy-start = (f32[1,128,3584]{2,1,0:T(8,128)S(1)}, f32[1,128,3584]{2,1,0:T(8,128)}, u32[]{:S(2)}) copy-start(f32[1,128,3584]{2,1,0:T(8,128)} %param.4) | copy-start | bytes 5505028
  2.2 1.2 %copy-start.2 = (bf16[1,128,3584]{2,1,0:T(8,128)(2,1)S(1)}, bf16[1,128,3584]{2,1,0:T(8,128)(2,1)}, u32[]{:S(2)}) copy-start(bf16[1,128,3584]{2,1,0:T(8,128)(2,1)} %param.3) | copy-start | bytes 2752516
  3.4 1.0 %copy-start.4 = (f32[3584,32]{0,1:T(8,128)S(1)}, f32[3584,32]{0,1:T(8,128)}, u32[]{:S(2)}) copy-start(f32[3584,32]{0,1:T(8,128)} %param.5) | copy-start | bytes 1376260
  4.4 25.2 %copy-start.1 = (f32[1,128,3584]{2,1,0:T(8,128)S(1)}, f32[1,128,3584]{2,1,0:T(8,128)}, u32[]{:S(2)}) copy-start(f32[1,128,3584]{2,1,0:T(8,128)} %param.4) | copy-start | bytes 5505028
  4.4 25.2 %copy-start.3 = (bf16[1,128,3584]{2,1,0:T(8,128)(2,1)S(1)}, bf16[1,128,3584]{2,1,0:T(8,128)(2,1)}, u32[]{:S(2)}) copy-start(bf16[1,128,3584]{2,1,0:T(8,128)(2,1)} %param.3) | copy-start | bytes 2752516
  7.9 21.7 %collective-permute-start = (f32[128,1792]{1,0:T(8,128)}, f32[128,1792]{1,0:T(8,128)}, u32[]{:S(2)}, u32[]{:S(2)}) collective-permute-start(f32[128,1792]{1,0:T(8,128)} %get-tuple-element.13), channel_id=1, source_target_pairs={{0,32},{32,0},{1,33},{33,1},{2,34},{34,2},{3,35},{35,3},{4,36},{36... | collective-permute-start | bytes 2752520 | tf_op jit(solution)/shard_map/ppermute | solution.py:228
  64.1 15.5 %all-to-all-start.3 = ((f32[32,16,128]{2,1,0:T(8,128)}), f32[32,16,128]{2,1,0:T(8,128)S(1)}, u32[]{:S(2)}, u32[]{:S(2)}) async-start(f32[32,16,128]{2,1,0:T(8,128)} %shard_map.61), calls=%async_computation.3 | async-start | bytes 524288 | tf_op jit(solution)/shard_map/all_to_all | solution.py:237

commit v3 on v2

v3 whole, which is shorter than its diff:
```python
import functools

import jax
import jax.numpy as jnp
from jax import lax
from jax.experimental import pallas as pl
from jax.experimental.pallas import tpu as pltpu
from jax.sharding import Mesh, PartitionSpec as P

F32, BF16 = jnp.float32, jnp.bfloat16
HIGHEST = lax.Precision.HIGHEST
DP = ("y", "core")
VOCAB = ("z", "x")
NY, NX, NZ = 8, 4, 8
RANK, ROWS, WIDTH = 32, 128, 3584
HALF = WIDTH // 2
LANES = 128
TILES = HALF // LANES
PIECE = TILES + 2
VMEM_LIMIT = 48 * 1024 * 1024
LEFT_CHUNKS = (1024, 1024, 1024, 512)
ANY = pl.BlockSpec(memory_space=pl.ANY)
VMEM = pl.BlockSpec(memory_space=pltpu.VMEM)

NT = (((1,), (1,)), ((), ()))
NN = (((1,), (0,)), ((), ()))


def split3(value):
    high = value.astype(BF16)
    rest = value - high.astype(F32)
    middle = rest.astype(BF16)
    low = (rest - middle.astype(F32)).astype(BF16)
    return high, middle, low


def dot(a, b, dims=NN):
    return lax.dot_general(a, b, dims, preferred_element_type=F32)


def stack_left(value):
    h, m, l = split3(value)
    return jnp.concatenate([h, h, m, m, h, l], axis=1)


def stack_right(value):
    h, m, l = split3(value)
    return jnp.concatenate([h, m, h, m, l, h], axis=0)


def kernel_call(body, out_shape, **options):
    return pl.pallas_call(
        body,
        out_shape=out_shape,
        compiler_params=pltpu.CompilerParams(vmem_limit_bytes=VMEM_LIMIT),
        **options,
    )


def vmem_call(body, out_shape):
    def call(*operands):
        return kernel_call(body, out_shape)(
            *(pltpu.with_memory_space_constraint(value, pltpu.VMEM) for value in operands)
        )

    return call


def shape(*dims):
    return jax.ShapeDtypeStruct(dims, F32)


def in_vmem(*dims, dtype=F32):
    return pltpu.VMEM(dims, dtype)


def left_body(grad_ref, error_ref, q_ref, p_ref, merged_ref, grad_buf, error_buf, q_buf, sems):
    plan, start = [], 0
    for at, size in enumerate(LEFT_CHUNKS):
        columns = pl.ds(start, size)
        copies = [
            pltpu.make_async_copy(ref.at[:, columns], buf.at[:, columns], sems.at[which, at])
            for which, (ref, buf) in enumerate(((grad_ref, grad_buf), (error_ref, error_buf), (q_ref, q_buf)))
        ]
        for copy in copies:
            copy.start()
        plan.append((slice(start, start + size), copies))
        start += size
    total = None
    for columns, copies in plan:
        for copy in copies:
            copy.wait()
        merged = grad_buf[:, columns].astype(F32) + error_buf[:, columns]
        merged_ref[:, columns] = merged
        left = jnp.concatenate(split3(q_buf[:, columns]), axis=0)
        right = jnp.concatenate(split3(merged), axis=0)
        product = dot(left, right, NT)
        total = product if total is None else total + product
    total = total[:RANK] + (total[RANK : 2 * RANK] + total[2 * RANK :])
    p_ref[...] = total[:, :ROWS] + (total[:, ROWS : 2 * ROWS] + total[:, 2 * ROWS :])


def left_product(grad, error, q_rows):
    return kernel_call(
        left_body,
        (in_vmem(RANK, ROWS), in_vmem(ROWS, WIDTH)),
        in_specs=[ANY] * 3,
        out_specs=(VMEM, VMEM),
        scratch_shapes=[
            pltpu.VMEM((ROWS, WIDTH), BF16),
            pltpu.VMEM((ROWS, WIDTH), F32),
            pltpu.VMEM((RANK, WIDTH), F32),
            pltpu.SemaphoreType.DMA((3, len(LEFT_CHUNKS))),
        ],
    )(*(pltpu.with_memory_space_constraint(value, pltpu.HBM) for value in (grad, error, q_rows)))


def right_body(mine_ref, parts_ref, chip_ref, pieces_ref, p_ref):
    p_sum = jnp.sum(parts_ref[...], axis=0)
    p_ref[...] = p_sum
    p_parts = jnp.concatenate(split3(p_sum), axis=0)
    h, m, l = split3(chip_ref[...])
    with_h = dot(p_parts, h)
    with_m = dot(p_parts[: 2 * RANK], m)
    with_l = dot(p_parts[:RANK], l)
    small = with_h[2 * RANK :] + with_m[RANK:] + with_l
    product = with_h[:RANK] + (with_h[RANK : 2 * RANK] + with_m[:RANK] + small)
    for tile in range(TILES):
        pieces_ref[:, tile, :] = product[:, tile * LANES : (tile + 1) * LANES]
    gram = lax.dot_general(p_sum, p_sum, NT, precision=HIGHEST, preferred_element_type=F32)
    packed = jnp.concatenate([gram[8 * a : 8 * a + 8] for a in range(4)], axis=1)
    row = jnp.sum(packed * mine_ref[...], axis=0, keepdims=True)
    pieces_ref[:, TILES, :] = jnp.broadcast_to(row, (RANK, LANES))
    pieces_ref[:, TILES + 1, :] = jnp.zeros((RANK, LANES), F32)


def right_product(mine, parts, chip_half):
    return vmem_call(right_body, (in_vmem(RANK, PIECE, LANES), in_vmem(RANK, ROWS)))(mine, parts, chip_half)


def plane_body(parts_ref, out_ref):
    rows = parts_ref[0]
    for member in range(1, NY * NX):
        rows += parts_ref[member]
    gram = [sum(parts_ref[y * NX + x, TILES : TILES + 1, :] for x in range(NX)) for y in range(NY)]
    both = jnp.concatenate([rows] + gram, axis=0)
    for z in range(NZ):
        out_ref[z] = both


def line_body(parts_ref, out_ref):
    rows = parts_ref[0, :PIECE, :]
    for z in range(1, NZ):
        rows += parts_ref[z, :PIECE, :]
    for member in range(NY * NX):
        out_ref[member] = rows


def factor_body(replicas, parts_ref, p_ref, basis_ref, basis_stack_ref, inverse_stack_ref):
    packed = parts_ref[0, PIECE:, :]
    for z in range(1, NZ):
        packed += parts_ref[z, PIECE:, :]
    gram = jnp.concatenate([packed[:, RANK * a : RANK * (a + 1)] for a in range(4)], axis=0)
    row = lax.broadcasted_iota(jnp.int32, (RANK, RANK), 0)
    column = lax.broadcasted_iota(jnp.int32, (RANK, RANK), 1)
    unit = jnp.where(row == column, 1.0, 0.0).astype(F32)
    work = jnp.concatenate([gram, unit], axis=1)
    below = lax.broadcasted_iota(jnp.int32, (RANK, 1), 0)
    inverse = []
    for j in range(RANK):
        pivot_row = work[j : j + 1, :]
        pivot = pivot_row[:, j : j + 1]
        inverse.append(pivot_row[:, RANK:] / jnp.sqrt(pivot))
        if j < RANK - 1:
            factor = jnp.where(below > j, work[:, j : j + 1] / pivot, 0.0)
            work = work - factor * pivot_row
    inverse = jnp.concatenate(inverse, axis=0)
    basis = lax.dot_general(inverse, p_ref[...], NN, precision=HIGHEST, preferred_element_type=F32)
    basis_ref[...] = basis
    basis_stack_ref[...] = stack_left(basis.T)
    inverse_stack_ref[...] = stack_left(inverse * (1.0 / replicas))


def final_body(parts_ref, inverse_ref, basis_ref, merged_ref, out_ref, q_ref, out_buf, q_buf, sems):
    copies = []
    for half in range(2):
        right = jnp.concatenate([parts_ref[half, :, tile, :] for tile in range(TILES)], axis=1)
        columns = slice(half * HALF, (half + 1) * HALF)
        q_new = dot(inverse_ref[...], stack_right(right))
        q_buf[:, columns] = q_new
        out_buf[:, columns] = merged_ref[:, columns] - dot(basis_ref[...], stack_right(q_new))
        for which, (buf, ref) in enumerate(((out_buf, out_ref), (q_buf, q_ref))):
            copies.append(pltpu.make_async_copy(buf.at[:, columns], ref.at[:, columns], sems.at[which, half]))
            copies[-1].start()
    for copy in copies:
        copy.wait()


def final(*operands):
    return kernel_call(
        final_body,
        (shape(ROWS, WIDTH), shape(RANK, WIDTH)),
        in_specs=[VMEM] * 4,
        out_specs=(ANY, ANY),
        scratch_shapes=[
            pltpu.VMEM((ROWS, WIDTH), F32),
            pltpu.VMEM((RANK, WIDTH), F32),
            pltpu.SemaphoreType.DMA((2, 2)),
        ],
    )(*(pltpu.with_memory_space_constraint(value, pltpu.VMEM) for value in operands))


def per_device(grad, error, q_prev):
    replicas = lax.axis_size(DP)
    core = lax.axis_index("core")
    mine = (lax.broadcasted_iota(jnp.int32, (8, LANES), 0) == lax.axis_index("y")).astype(F32)

    p_local, merged = left_product(grad[0], error[0], q_prev.T)
    given = lax.dynamic_slice_in_dim(merged, (1 - core) * HALF, HALF, axis=1)
    own_half = lax.dynamic_slice_in_dim(merged, core * HALF, HALF, axis=1)
    p_both = lax.all_gather(p_local, "core")
    p_both, given, mine = lax.optimization_barrier((p_both, given, mine))
    taken = lax.ppermute(given, "core", [(0, 1), (1, 0)])
    p_chip = jnp.sum(p_both, axis=0)
    p_parts = lax.all_to_all(jnp.broadcast_to(p_chip[None], (NY, RANK, ROWS)), "y", 0, 0)

    pieces, p_sum = right_product(mine, p_parts, own_half + taken)
    pieces = lax.all_to_all(pieces, ("y", "x"), 0, 0)
    lines = vmem_call(plane_body, in_vmem(NZ, PIECE + 8, LANES))(pieces)
    lines = lax.all_to_all(lines, "z", 0, 0)
    own = vmem_call(line_body, in_vmem(NY * NX, PIECE, LANES))(lines)
    own = lax.all_to_all(own, ("y", "x"), 0, 0)
    basis, basis_stack, inverse_stack = vmem_call(
        functools.partial(factor_body, replicas),
        (shape(RANK, ROWS), in_vmem(ROWS, 6 * RANK, dtype=BF16), in_vmem(RANK, 6 * RANK, dtype=BF16)),
    )(lines, p_sum)
    whole = lax.all_gather(own, "core")
    new_error, q_new = final(whole, inverse_stack, basis_stack, merged)
    return (new_error[None], basis.T, q_new.T)


def solution(mesh):
    fine = Mesh(mesh.devices.reshape(NY, 2, NZ, NX), DP + VOCAB)
    placed = (P(DP, VOCAB, None), P(DP, VOCAB, None), P())
    return jax.shard_map(
        per_device,
        mesh=fine,
        in_specs=placed,
        out_specs=(P(DP, VOCAB, None), P(VOCAB, None), P()),
        check_vma=False,
    )
```

time: 88.6 us -> 83 us (0.937)
  waiting for transfers between devices: 6.94 us -> 14.2 us
  blocking collectives: 50.7 us -> 45.2 us
  starting transfers between devices: 13.9 us -> 10.9 us
  local copies, waits for them, and re-layouts: 3.72 us -> 0.79 us
  Pallas kernels: 12.1 us -> 9.36 us
  other arithmetic: 0.08 us -> 1.33 us
    all_to_all x1 -> x0, blocking collectives: 10.8 us -> none  [per_device(): lax.all_to_all(jnp.broadcast_to(p_chip[None], (NY, RANK, ROWS)), 'y', 0, 0)]
    all_to_all x0 -> x1, waiting for transfers between devices: none -> 7.21 us  [per_device(): lax.all_to_all(jnp.broadcast_to(p_chip[None], (NY, RANK, ROWS)), 'y', 0, 0)]
    ppermute x1, starting transfers between devices: 8.78 us -> 2.24 us  [per_device(): taken = lax.ppermute(given, 'core', [(0, 1), (1, 0)])]
    all_gather x1, blocking collectives: 2.11 us -> 8.37 us  [per_device(): p_both = lax.all_gather(p_local, 'core')]
    unnamed x10 -> x0, local copies, waits for them, and re-layouts: 3.7 us -> none
    all_to_all x0 -> x1, starting transfers between devices: none -> 3.37 us  [per_device(): lax.all_to_all(jnp.broadcast_to(p_chip[None], (NY, RANK, ROWS)), 'y', 0, 0)]
    pallas_call x6, Pallas kernels: 12.1 us -> 9.36 us  [the longest x4 4.72 us: call(): kernel_call(body, out_shape)]
    add x0 -> x1, other arithmetic: none -> 1.32 us  [per_device(): pieces, p_sum = right_product(mine, p_parts, own_half + taken)]
  transfers between devices with their start and end apart: 2 -> 3, of which waited for: 1 -> 2; matrix products, arithmetic and copies ran while one was open for 0% -> 2% of each run, Pallas kernels for 4% -> 4%
where the time goes in v3:
time: 83 us; the launch traced here: 82.6 us
  blocking collectives  45.2 us (54%)
  waiting for transfers between devices  14.2 us (17%)
  starting transfers between devices  10.9 us (13%)
  Pallas kernels  9.36 us (11%)
  other arithmetic  1.33 us (2%)
    all_to_all x1, blocking collectives, per_device(): lines = lax.all_to_all(lines, 'z', 0, 0)  17.3 us
    all_to_all x1, blocking collectives, per_device(): pieces = lax.all_to_all(pieces, ('y', 'x'), 0, 0)  13.3 us
    all_gather x1, blocking collectives, per_device(): p_both = lax.all_gather(p_local, 'core')  8.37 us
    all_to_all x1, waiting for transfers between devices, per_device(): lax.all_to_all(jnp.broadcast_to(p_chip[None], (NY, RANK, ROWS)), 'y', 0, 0)  7.21 us
    all_to_all x1, waiting for transfers between devices, per_device(): own = lax.all_to_all(own, ('y', 'x'), 0, 0)  6.97 us
    all_gather x1, blocking collectives, per_device(): whole = lax.all_gather(own, 'core')  6.22 us
    all_to_all x1, starting transfers between devices, per_device(): own = lax.all_to_all(own, ('y', 'x'), 0, 0)  5.34 us
    pallas_call x4, Pallas kernels, call(): kernel_call(body, out_shape)  4.72 us
  transfers between devices with their start and end apart: 3, of which 2 were waited for; matrix products, arithmetic and copies ran while one was open for 2% of the time, Pallas kernels for 4%

profile of v3, /device:TPU:1, one launch (start us, length us, event | category | flops | bytes accessed | tf_op | source)
XLA Modules:
  0.0 82.6 jit_solution(15969033464889377078)
XLA Ops:
  0.6 2.7 %shard_map.58 = (f32[32,128]{1,0:T(8,128)S(1)}, f32[128,3584]{1,0:T(8,128)S(1)}) custom-call(bf16[128,3584]{1,0:T(8,128)(2,1)} %bitcast.10, f32[128,3584]{1,0:T(8,128)} %bitcast.9, f32[32,3584]{1,0:T(8,128)} %bitcast.11), custom_call_target="tpu_custom_call" | custom-call | tf_op jit(solution)/shard_map/pallas_call | solution.py:104
  3.4 8.4 %all-gather = f32[64,128]{1,0:T(8,128)S(1)} all-gather(f32[32,128]{1,0:T(8,128)S(1)} %get-tuple-element.15), channel_id=2, replica_groups=mesh['y'=8,'core'=2,'z'=8,'x'=4] {'core'}, dimensions={0}, use_global_device_ids=true | all-gather | bytes 49152 | tf_op jit(solution)/shard_map/all_gather | solution.py:221
  11.7 0.1 constant_dynamic-slice_fusion
  11.8 0.1 iota.7.mine_ref
  11.9 2.2 %collective-permute-start = (f32[128,1792]{1,0:T(8,128)S(1)}, f32[128,1792]{1,0:T(8,128)}, u32[]{:S(2)}, u32[]{:S(2)}) collective-permute-start(f32[128,1792]{1,0:T(8,128)S(1)} %constant_dynamic-slice_fusion), channel_id=1, source_target_pairs={{0,32},{32,0},{1,33},{33,1},{2,34},{34,2},{3,35},{35,3},{4,36},{36... | collective-permute-start | bytes 2752520 | tf_op jit(solution)/shard_map/ppermute | solution.py:223
  14.1 0.7 broadcast_in_dim.4
  14.8 3.4 %all-to-all-start = ((f32[8,32,128]{2,1,0:T(8,128)}), f32[8,32,128]{2,1,0:T(8,128)S(1)}, u32[]{:S(2)}, u32[]{:S(2)}) async-start(f32[8,32,128]{2,1,0:T(8,128)} %broadcast_in_dim.4), calls=%async_computation | async-start | bytes 262144 | tf_op jit(solution)/shard_map/all_to_all | solution.py:225
  18.2 0.0 collective-permute-done
  18.2 1.3 %dynamic-slice_add_fusion.chip_ref = f32[128,1792]{1,0:T(8,128)S(1)} fusion(f32[128,1792]{1,0:T(8,128)} %collective-permute-done, f32[128,3584]{1,0:T(8,128)S(1)} %get-tuple-element.16.merged_ref, s32[]{:T(128)S(6)} %select_n.7), kind=kLoop, calls=%fused_computation | loop fusion | flops 229376 | bytes 2752516 | tf_op jit(solution)/shard_map/add | solution.py:227
  19.5 7.2 %all-to-all-done.parts_ref = f32[8,32,128]{2,1,0:T(8,128)S(1)} async-done(((f32[8,32,128]{2,1,0:T(8,128)}), f32[8,32,128]{2,1,0:T(8,128)S(1)}, u32[]{:S(2)}, u32[]{:S(2)}) %all-to-all-start) | async-done | bytes 131104 | tf_op jit(solution)/shard_map/all_to_all | solution.py:225
  26.7 0.5 shard_map.59
  27.2 13.3 %all_to_all.20.parts_ref = f32[32,16,128]{2,1,0:T(8,128)S(1)} all-to-all(f32[32,16,128]{2,1,0:T(8,128)S(1)} %get-tuple-element.20), channel_id=1, replica_groups=mesh['y'=8,'core'=2,'z'=8,'x'=4] {'y','x'}, dimensions={0} | all-to-all | bytes 524288 | tf_op jit(solution)/shard_map/all_to_all | solution.py:228
  40.6 17.3 %all_to_all.21.parts_ref = f32[8,24,128]{2,1,0:T(8,128)S(1)} all-to-all(f32[8,24,128]{2,1,0:T(8,128)S(1)} %shard_map.60), channel_id=1, replica_groups=mesh['y'=8,'core'=2,'z'=8,'x'=4] {'z'}, dimensions={0} | all-to-all | bytes 196608 | tf_op jit(solution)/shard_map/all_to_all | solution.py:230
  57.9 0.7 shard_map.61
  58.6 5.3 %all-to-all-start.3 = ((f32[32,16,128]{2,1,0:T(8,128)}), f32[32,16,128]{2,1,0:T(8,128)S(1)}, u32[]{:S(2)}, u32[]{:S(2)}) async-start(f32[32,16,128]{2,1,0:T(8,128)} %shard_map.61), calls=%async_computation.3 | async-start | bytes 524288 | tf_op jit(solution)/shard_map/all_to_all | solution.py:232
  64.0 3.5 %shard_map.62 = (f32[32,128]{1,0:T(8,128)}, bf16[128,192]{1,0:T(8,128)(2,1)S(1)}, bf16[32,192]{1,0:T(8,128)(2,1)S(1)}) custom-call(f32[8,24,128]{2,1,0:T(8,128)S(1)} %all_to_all.21.parts_ref, f32[32,128]{1,0:T(8,128)S(1)} %get-tuple-element.21.p_ref), custom_call_target="tpu_custom_call" | custom-call | tf_op jit(solution)/shard_map/pallas_call | solution.py:62
  67.4 7.0 %all-to-all-done.3 = f32[32,16,128]{2,1,0:T(8,128)S(1)} async-done(((f32[32,16,128]{2,1,0:T(8,128)}), f32[32,16,128]{2,1,0:T(8,128)S(1)}, u32[]{:S(2)}, u32[]{:S(2)}) %all-to-all-start.3) | async-done | bytes 262176 | tf_op jit(solution)/shard_map/all_to_all | solution.py:232
  74.4 6.2 %all-gather.1 = f32[64,16,128]{2,1,0:T(8,128)S(1)} all-gather(f32[32,16,128]{2,1,0:T(8,128)S(1)} %all-to-all-done.3), channel_id=3, replica_groups=mesh['y'=8,'core'=2,'z'=8,'x'=4] {'core'}, dimensions={0}, use_global_device_ids=true | all-gather | bytes 786432 | tf_op jit(solution)/shard_map/all_gather | solution.py:237
  80.6 1.9 %shard_map.63 = (f32[128,3584]{1,0:T(8,128)}, f32[32,3584]{1,0:T(8,128)}) custom-call(f32[2,32,16,128]{3,2,1,0:T(8,128)S(1)} %bitcast.8, bf16[32,192]{1,0:T(8,128)(2,1)S(1)} %get-tuple-element.22.inverse_ref, bf16[128,192]{1,0:T(8,128)(2,1)S(1)} %get-tuple-element.23.basis_ref, f32[128,3584]{1,0:T(8,128)S(1)} %get-tuple-element.16.merged_ref), custom_call_target="tpu_custom_call" | custom-call | tf_op jit(solution)/shard_map/pallas_call | solution.py:200
  (3 shorter events, 0.0 us)
Async XLA Ops:
  11.9 6.3 %collective-permute-start = (f32[128,1792]{1,0:T(8,128)S(1)}, f32[128,1792]{1,0:T(8,128)}, u32[]{:S(2)}, u32[]{:S(2)}) collective-permute-start(f32[128,1792]{1,0:T(8,128)S(1)} %constant_dynamic-slice_fusion), channel_id=1, source_target_pairs={{0,32},{32,0},{1,33},{33,1},{2,34},{34,2},{3,35},{35,3},{4,36},{36... | collective-permute-start | bytes 2752520 | tf_op jit(solution)/shard_map/ppermute | solution.py:223
  14.8 11.9 %all-to-all-start = ((f32[8,32,128]{2,1,0:T(8,128)}), f32[8,32,128]{2,1,0:T(8,128)S(1)}, u32[]{:S(2)}, u32[]{:S(2)}) async-start(f32[8,32,128]{2,1,0:T(8,128)} %broadcast_in_dim.4), calls=%async_computation | async-start | bytes 262144 | tf_op jit(solution)/shard_map/all_to_all | solution.py:225
  58.6 15.8 %all-to-all-start.3 = ((f32[32,16,128]{2,1,0:T(8,128)}), f32[32,16,128]{2,1,0:T(8,128)S(1)}, u32[]{:S(2)}, u32[]{:S(2)}) async-start(f32[32,16,128]{2,1,0:T(8,128)} %shard_map.61), calls=%async_computation.3 | async-start | bytes 524288 | tf_op jit(solution)/shard_map/all_to_all | solution.py:232

commit v4 on v3

--- a/solution.py
+++ b/solution.py
@@ -9,9 +9,14 @@
 
 F32, BF16 = jnp.float32, jnp.bfloat16
 HIGHEST = lax.Precision.HIGHEST
-DP = ("y", "core")
-VOCAB = ("z", "x")
 NY, NX, NZ = 8, 4, 8
+Y = ("y2", "y1", "y0")
+Z = ("z2", "z1", "z0")
+Y_FAR_FIRST = ("y1", "y0", "y2")
+Z_FAR_FIRST = ("z1", "z0", "z2")
+DP = Y + ("core",)
+VOCAB = Z + ("x",)
+PLANE = Y + ("x",)
 RANK, ROWS, WIDTH = 32, 128, 3584
 HALF = WIDTH // 2
 LANES = 128
@@ -115,27 +120,28 @@
     )(*(pltpu.with_memory_space_constraint(value, pltpu.HBM) for value in (grad, error, q_rows)))
 
 
-def right_body(mine_ref, parts_ref, chip_ref, pieces_ref, p_ref):
+def right_body(mine_ref, parts_ref, merged_ref, pieces_ref, p_ref):
     p_sum = jnp.sum(parts_ref[...], axis=0)
     p_ref[...] = p_sum
     p_parts = jnp.concatenate(split3(p_sum), axis=0)
-    h, m, l = split3(chip_ref[...])
-    with_h = dot(p_parts, h)
-    with_m = dot(p_parts[: 2 * RANK], m)
-    with_l = dot(p_parts[:RANK], l)
-    small = with_h[2 * RANK :] + with_m[RANK:] + with_l
-    product = with_h[:RANK] + (with_h[RANK : 2 * RANK] + with_m[:RANK] + small)
-    for tile in range(TILES):
-        pieces_ref[:, tile, :] = product[:, tile * LANES : (tile + 1) * LANES]
     gram = lax.dot_general(p_sum, p_sum, NT, precision=HIGHEST, preferred_element_type=F32)
     packed = jnp.concatenate([gram[8 * a : 8 * a + 8] for a in range(4)], axis=1)
-    row = jnp.sum(packed * mine_ref[...], axis=0, keepdims=True)
-    pieces_ref[:, TILES, :] = jnp.broadcast_to(row, (RANK, LANES))
-    pieces_ref[:, TILES + 1, :] = jnp.zeros((RANK, LANES), F32)
-
-
-def right_product(mine, parts, chip_half):
-    return vmem_call(right_body, (in_vmem(RANK, PIECE, LANES), in_vmem(RANK, ROWS)))(mine, parts, chip_half)
+    row = 0.5 * jnp.sum(packed * mine_ref[...], axis=0, keepdims=True)
+    for half in range(2):
+        h, m, l = split3(merged_ref[:, half * HALF : (half + 1) * HALF])
+        with_h = dot(p_parts, h)
+        with_m = dot(p_parts[: 2 * RANK], m)
+        with_l = dot(p_parts[:RANK], l)
+        small = with_h[2 * RANK :] + with_m[RANK:] + with_l
+        product = with_h[:RANK] + (with_h[RANK : 2 * RANK] + with_m[:RANK] + small)
+        for tile in range(TILES):
+            pieces_ref[half, :, tile, :] = product[:, tile * LANES : (tile + 1) * LANES]
+        pieces_ref[half, :, TILES, :] = jnp.broadcast_to(row, (RANK, LANES))
+        pieces_ref[half, :, TILES + 1, :] = jnp.zeros((RANK, LANES), F32)
+
+
+def right_product(mine, parts, merged):
+    return vmem_call(right_body, (in_vmem(2, RANK, PIECE, LANES), in_vmem(RANK, ROWS)))(mine, parts, merged)
 
 
 def plane_body(parts_ref, out_ref):
@@ -210,26 +216,28 @@
     )(*(pltpu.with_memory_space_constraint(value, pltpu.VMEM) for value in operands))
 
 
+def pick(values, at):
+    return lax.dynamic_index_in_dim(values, at, keepdims=False)
+
+
 def per_device(grad, error, q_prev):
     replicas = lax.axis_size(DP)
-    core = lax.axis_index("core")
-    mine = (lax.broadcasted_iota(jnp.int32, (8, LANES), 0) == lax.axis_index("y")).astype(F32)
+    core = lax.axis_index("core").astype(jnp.uint32)
+    mine = (lax.broadcasted_iota(jnp.int32, (8, LANES), 0) == lax.axis_index(Y)).astype(F32)
 
     p_local, merged = left_product(grad[0], error[0], q_prev.T)
-    given = lax.dynamic_slice_in_dim(merged, (1 - core) * HALF, HALF, axis=1)
-    own_half = lax.dynamic_slice_in_dim(merged, core * HALF, HALF, axis=1)
-    p_both = lax.all_gather(p_local, "core")
-    p_both, given, mine = lax.optimization_barrier((p_both, given, mine))
-    taken = lax.ppermute(given, "core", [(0, 1), (1, 0)])
+    p_both, mine, core, other = lax.optimization_barrier((lax.all_gather(p_local, "core"), mine, core, 1 - core))
     p_chip = jnp.sum(p_both, axis=0)
-    p_parts = lax.all_to_all(jnp.broadcast_to(p_chip[None], (NY, RANK, ROWS)), "y", 0, 0)
-
-    pieces, p_sum = right_product(mine, p_parts, own_half + taken)
-    pieces = lax.all_to_all(pieces, ("y", "x"), 0, 0)
+    p_parts = lax.all_to_all(jnp.broadcast_to(p_chip[None], (NY, RANK, ROWS)), Y_FAR_FIRST, 0, 0)
+
+    pieces, p_sum = right_product(mine, p_parts, merged)
+    traded = lax.all_gather(pick(pieces, other), "core")
+    pieces = pick(pieces, core) + pick(traded, other)
+    pieces = lax.all_to_all(pieces, PLANE, 0, 0)
     lines = vmem_call(plane_body, in_vmem(NZ, PIECE + 8, LANES))(pieces)
-    lines = lax.all_to_all(lines, "z", 0, 0)
+    lines = lax.all_to_all(lines, Z_FAR_FIRST, 0, 0)
     own = vmem_call(line_body, in_vmem(NY * NX, PIECE, LANES))(lines)
-    own = lax.all_to_all(own, ("y", "x"), 0, 0)
+    own = lax.all_to_all(own, PLANE, 0, 0)
     basis, basis_stack, inverse_stack = vmem_call(
         functools.partial(factor_body, replicas),
         (shape(RANK, ROWS), in_vmem(ROWS, 6 * RANK, dtype=BF16), in_vmem(RANK, 6 * RANK, dtype=BF16)),
@@ -240,7 +248,7 @@
 
 
 def solution(mesh):
-    fine = Mesh(mesh.devices.reshape(NY, 2, NZ, NX), DP + VOCAB)
+    fine = Mesh(mesh.devices.reshape(2, 2, 2, 2, 2, 2, 2, NX), DP + VOCAB)
     placed = (P(DP, VOCAB, None), P(DP, VOCAB, None), P())
     return jax.shard_map(
         per_device,

time: 83 us -> 82.6 us (level)
  blocking collectives: 45.2 us -> 60.1 us
  waiting for transfers between devices: 14.2 us -> 6.94 us
  starting transfers between devices: 10.9 us -> 4.69 us
  other arithmetic: 1.33 us -> 0.04 us
    all_to_all x2 -> x3, blocking collectives: 30.7 us -> 41.9 us  [the longest x1 16.5 us: per_device(): lines = lax.all_to_all(lines, Z_FAR_FIRST, 0, 0)]
    all_to_all x2 -> x1, waiting for transfers between devices: 14.2 us -> 6.94 us  [per_device(): own = lax.all_to_all(own, PLANE, 0, 0)]
    all_to_all x2 -> x1, starting transfers between devices: 8.71 us -> 4.69 us  [per_device(): own = lax.all_to_all(own, PLANE, 0, 0)]
    all_gather x1 -> x2, blocking collectives: 8.37 us -> 11.8 us  [the longest x1 8.37 us: per_device(): lax.all_gather(p_local, 'core')]
    ppermute x1 -> x0, starting transfers between devices: 2.24 us -> none  [per_device(): taken = lax.ppermute(given, 'core', [(0, 1), (1, 0)])]
    add x1, other arithmetic: 1.32 us -> 0.03 us  [per_device(): pieces = pick(pieces, core) + pick(traded, other)]
  transfers between devices with their start and end apart: 3 -> 1, of which waited for: 2 -> 1; matrix products, arithmetic and copies ran while one was open for 2% -> 0% of each run, Pallas kernels for 4% -> 4%
where the time goes in v4:
time: 82.6 us; the launch traced here: 82.3 us
  blocking collectives  60.1 us (73%)
  Pallas kernels  9.71 us (12%)
  waiting for transfers between devices  6.94 us (8%)
  starting transfers between devices  4.69 us (6%)
    all_to_all x1, blocking collectives, per_device(): lines = lax.all_to_all(lines, Z_FAR_FIRST, 0, 0)  16.5 us
    all_to_all x1, blocking collectives, per_device(): pieces = lax.all_to_all(pieces, PLANE, 0, 0)  16.2 us
    all_to_all x1, blocking collectives, per_device(): lax.all_to_all(jnp.broadcast_to(p_chip[None], (NY, RANK, ROWS)), Y_FAR_FI...  9.19 us
    all_gather x1, blocking collectives, per_device(): lax.all_gather(p_local, 'core')  8.37 us
    all_to_all x1, waiting for transfers between devices, per_device(): own = lax.all_to_all(own, PLANE, 0, 0)  6.94 us
    all_gather x1, blocking collectives, per_device(): whole = lax.all_gather(own, 'core')  6.36 us
    pallas_call x4, Pallas kernels, call(): kernel_call(body, out_shape)  5.08 us
    all_to_all x1, starting transfers between devices, per_device(): own = lax.all_to_all(own, PLANE, 0, 0)  4.69 us
  transfers between devices with their start and end apart: 1, of which 1 were waited for; matrix products, arithmetic and copies ran while one was open for 0% of the time, Pallas kernels for 4%

profile of v4, /device:TPU:1, one launch (start us, length us, event | category | flops | bytes accessed | tf_op | source)
XLA Modules:
  0.0 82.3 jit_solution(10024643872530232649)
XLA Ops:
  0.7 2.7 %shard_map.58 = (f32[32,128]{1,0:T(8,128)S(1)}, f32[128,3584]{1,0:T(8,128)S(1)}) custom-call(bf16[128,3584]{1,0:T(8,128)(2,1)} %bitcast.12, f32[128,3584]{1,0:T(8,128)} %bitcast.11, f32[32,3584]{1,0:T(8,128)} %bitcast.13), custom_call_target="tpu_custom_call" | custom-call | tf_op jit(solution)/shard_map/pallas_call | solution.py:109
  3.4 8.4 %all-gather = f32[64,128]{1,0:T(8,128)S(1)} all-gather(f32[32,128]{1,0:T(8,128)S(1)} %get-tuple-element.16), channel_id=2, replica_groups=mesh['y2'=2,'y1'=2,'y0'=2,'core'=2,'z2'=2,'z1'=2,'z0'=2,'x'=4] {'core'}, dimensions={0}, use_global_device_ids=true | all-gather | bytes 49152 | tf_op jit(solution)/shard_map/all_gather | solution.py:229
  11.7 0.1 iota.7.mine_ref
  11.8 9.2 %all_to_all.20.parts_ref = f32[8,32,128]{2,1,0:T(8,128)S(1)} all-to-all(f32[8,32,128]{2,1,0:T(8,128)S(1)} %broadcast_in_dim.4), channel_id=1, replica_groups=mesh['y2'=2,'y1'=2,'y0'=2,'core'=2,'z2'=2,'z1'=2,'z0'=2,'x'=4] {'y1','y0..., dimensions={0} | all-to-all | bytes 262144 | tf_op jit(solution)/shard_map/all_to_all | solution.py:231
  21.0 0.9 %shard_map.59 = (f32[2,32,16,128]{3,2,1,0:T(8,128)S(1)}, f32[32,128]{1,0:T(8,128)S(1)}) custom-call(f32[8,128]{1,0:T(8,128)S(1)} %iota.7.mine_ref, f32[8,32,128]{2,1,0:T(8,128)S(1)} %all_to_all.20.parts_ref, f32[128,3584]{1,0:T(8,128)S(1)} %get-tuple-element.19.merged_ref), custom_call_target="tpu_custom_call" | custom-call | tf_op jit(solution)/shard_map/pallas_call | solution.py:67
  21.9 3.5 %all_gather.18 = f32[2,32,16,128]{3,2,1,0:T(8,128)S(1)} all-gather(f32[1,32,16,128]{3,2,1,0:T(8,128)S(1)} %constant_dynamic-slice_fusion), channel_id=1, replica_groups=mesh['y2'=2,'y1'=2,'y0'=2,'core'=2,'z2'=2,'z1'=2,'z0'=2,'x'=4] {'core'}, dimensions={0}, use_global_device_ids=true | all-gather | bytes 786432 | tf_op jit(solution)/shard_map/all_gather | solution.py:234
  25.4 16.2 %all_to_all.21.parts_ref = f32[32,16,128]{2,1,0:T(8,128)S(1)} all-to-all(f32[32,16,128]{2,1,0:T(8,128)S(1)} %add_bitcast_fusion), channel_id=1, replica_groups=mesh['y2'=2,'y1'=2,'y0'=2,'core'=2,'z2'=2,'z1'=2,'z0'=2,'x'=4] {'y2','y1..., dimensions={0} | all-to-all | bytes 524288 | tf_op jit(solution)/shard_map/all_to_all | solution.py:236
  41.7 16.5 %all_to_all.22.parts_ref = f32[8,24,128]{2,1,0:T(8,128)S(1)} all-to-all(f32[8,24,128]{2,1,0:T(8,128)S(1)} %shard_map.60), channel_id=1, replica_groups=mesh['y2'=2,'y1'=2,'y0'=2,'core'=2,'z2'=2,'z1'=2,'z0'=2,'x'=4] {'z1','z0..., dimensions={0} | all-to-all | bytes 196608 | tf_op jit(solution)/shard_map/all_to_all | solution.py:238
  58.2 0.7 shard_map.61
  58.9 4.7 %all-to-all-start.3 = ((f32[32,16,128]{2,1,0:T(8,128)}), f32[32,16,128]{2,1,0:T(8,128)S(1)}, u32[]{:S(2)}, u32[]{:S(2)}) async-start(f32[32,16,128]{2,1,0:T(8,128)} %shard_map.61), calls=%async_computation.3 | async-start | bytes 524288 | tf_op jit(solution)/shard_map/all_to_all | solution.py:240
  63.6 3.5 %shard_map.62 = (f32[32,128]{1,0:T(8,128)}, bf16[128,192]{1,0:T(8,128)(2,1)S(1)}, bf16[32,192]{1,0:T(8,128)(2,1)S(1)}) custom-call(f32[8,24,128]{2,1,0:T(8,128)S(1)} %all_to_all.22.parts_ref, f32[32,128]{1,0:T(8,128)S(1)} %get-tuple-element.23.p_ref), custom_call_target="tpu_custom_call" | custom-call | tf_op jit(solution)/shard_map/pallas_call | solution.py:67
  67.1 6.9 %all-to-all-done.3 = f32[32,16,128]{2,1,0:T(8,128)S(1)} async-done(((f32[32,16,128]{2,1,0:T(8,128)}), f32[32,16,128]{2,1,0:T(8,128)S(1)}, u32[]{:S(2)}, u32[]{:S(2)}) %all-to-all-start.3) | async-done | bytes 262176 | tf_op jit(solution)/shard_map/all_to_all | solution.py:240
  74.0 6.4 %all-gather.1 = f32[64,16,128]{2,1,0:T(8,128)S(1)} all-gather(f32[32,16,128]{2,1,0:T(8,128)S(1)} %all-to-all-done.3), channel_id=3, replica_groups=mesh['y2'=2,'y1'=2,'y0'=2,'core'=2,'z2'=2,'z1'=2,'z0'=2,'x'=4] {'core'}, dimensions={0}, use_global_device_ids=true | all-gather | bytes 786432 | tf_op jit(solution)/shard_map/all_gather | solution.py:245
  80.4 1.9 %shard_map.63 = (f32[128,3584]{1,0:T(8,128)}, f32[32,3584]{1,0:T(8,128)}) custom-call(f32[2,32,16,128]{3,2,1,0:T(8,128)S(1)} %bitcast.10, bf16[32,192]{1,0:T(8,128)(2,1)S(1)} %get-tuple-element.24.inverse_ref, bf16[128,192]{1,0:T(8,128)(2,1)S(1)} %get-tuple-element.25.basis_ref, f32[128,3584]{1,0:T(8,128)S(1)} %get-tuple-element.19.merged_ref), custom_call_target="tpu_custom_call" | custom-call | tf_op jit(solution)/shard_map/pallas_call | solution.py:206
  (6 shorter events, 0.1 us)
Async XLA Ops:
  58.9 15.1 %all-to-all-start.3 = ((f32[32,16,128]{2,1,0:T(8,128)}), f32[32,16,128]{2,1,0:T(8,128)S(1)}, u32[]{:S(2)}, u32[]{:S(2)}) async-start(f32[32,16,128]{2,1,0:T(8,128)} %shard_map.61), calls=%async_computation.3 | async-start | bytes 524288 | tf_op jit(solution)/shard_map/all_to_all | solution.py:240

commit v5 on v4

--- a/solution.py
+++ b/solution.py
@@ -5,18 +5,34 @@
 from jax import lax
 from jax.experimental import pallas as pl
 from jax.experimental.pallas import tpu as pltpu
-from jax.sharding import Mesh, PartitionSpec as P
+from jax.sharding import PartitionSpec as P
 
 F32, BF16 = jnp.float32, jnp.bfloat16
 HIGHEST = lax.Precision.HIGHEST
-NY, NX, NZ = 8, 4, 8
-Y = ("y2", "y1", "y0")
-Z = ("z2", "z1", "z0")
-Y_FAR_FIRST = ("y1", "y0", "y2")
-Z_FAR_FIRST = ("z1", "z0", "z2")
-DP = Y + ("core",)
-VOCAB = Z + ("x",)
-PLANE = Y + ("x",)
+AXES = ("dp", "vocab")
+RING, NX = 8, 4
+PLANE = RING * NX
+
+
+def device(y, core, z, x):
+    return ((y * 2 + core) * RING + z) * NX + x
+
+
+FAR_FIRST = (0, 4, 1, 5, 2, 6, 3, 7)
+CHIP_GROUPS = [[device(y, c, z, x) for c in range(2)] for y in range(RING) for z in range(RING) for x in range(NX)]
+Y_GROUPS = [[device(y, c, z, x) for y in FAR_FIRST] for c in range(2) for z in range(RING) for x in range(NX)]
+
+
+def across(core, a, b, x):
+    return device(b, core, a, x) if core else device(a, core, b, x)
+
+
+PLANE_GROUPS = [
+    [across(c, a, b, x) for a in range(RING) for x in range(NX)] for c in range(2) for b in range(RING)
+]
+LINE_GROUPS = [
+    [across(c, a, b, x) for b in FAR_FIRST] for c in range(2) for a in range(RING) for x in range(NX)
+]
 RANK, ROWS, WIDTH = 32, 128, 3584
 HALF = WIDTH // 2
 LANES = 128
@@ -120,13 +136,13 @@
     )(*(pltpu.with_memory_space_constraint(value, pltpu.HBM) for value in (grad, error, q_rows)))
 
 
-def right_body(mine_ref, parts_ref, merged_ref, pieces_ref, p_ref):
+def right_body(place_ref, parts_ref, merged_ref, pieces_ref, p_ref):
     p_sum = jnp.sum(parts_ref[...], axis=0)
     p_ref[...] = p_sum
     p_parts = jnp.concatenate(split3(p_sum), axis=0)
     gram = lax.dot_general(p_sum, p_sum, NT, precision=HIGHEST, preferred_element_type=F32)
     packed = jnp.concatenate([gram[8 * a : 8 * a + 8] for a in range(4)], axis=1)
-    row = 0.5 * jnp.sum(packed * mine_ref[...], axis=0, keepdims=True)
+    row = 0.5 * jnp.sum(packed * place_ref[:8, :], axis=0, keepdims=True)
     for half in range(2):
         h, m, l = split3(merged_ref[:, half * HALF : (half + 1) * HALF])
         with_h = dot(p_parts, h)
@@ -140,32 +156,36 @@
         pieces_ref[half, :, TILES + 1, :] = jnp.zeros((RANK, LANES), F32)
 
 
-def right_product(mine, parts, merged):
-    return vmem_call(right_body, (in_vmem(2, RANK, PIECE, LANES), in_vmem(RANK, ROWS)))(mine, parts, merged)
-
-
-def plane_body(parts_ref, out_ref):
+def right_product(place, parts, merged):
+    return vmem_call(right_body, (in_vmem(2, RANK, PIECE, LANES), in_vmem(RANK, ROWS)))(place, parts, merged)
+
+
+def plane_body(place_ref, parts_ref, out_ref):
     rows = parts_ref[0]
-    for member in range(1, NY * NX):
+    for member in range(1, PLANE):
         rows += parts_ref[member]
-    gram = [sum(parts_ref[y * NX + x, TILES : TILES + 1, :] for x in range(NX)) for y in range(NY)]
-    both = jnp.concatenate([rows] + gram, axis=0)
-    for z in range(NZ):
-        out_ref[z] = both
+    apart = [sum(parts_ref[a * NX + x, TILES : TILES + 1, :] for x in range(NX)) for a in range(RING)]
+    total = apart[FAR_FIRST[0]]
+    for z in FAR_FIRST[1:]:
+        total += apart[z]
+    gram = jnp.where(place_ref[8:, :] > 0, total * place_ref[:8, :], jnp.concatenate(apart, axis=0))
+    both = jnp.concatenate([rows, gram], axis=0)
+    for member in range(RING):
+        out_ref[member] = both
 
 
 def line_body(parts_ref, out_ref):
     rows = parts_ref[0, :PIECE, :]
-    for z in range(1, NZ):
-        rows += parts_ref[z, :PIECE, :]
-    for member in range(NY * NX):
+    for member in range(1, RING):
+        rows += parts_ref[member, :PIECE, :]
+    for member in range(PLANE):
         out_ref[member] = rows
 
 
 def factor_body(replicas, parts_ref, p_ref, basis_ref, basis_stack_ref, inverse_stack_ref):
     packed = parts_ref[0, PIECE:, :]
-    for z in range(1, NZ):
-        packed += parts_ref[z, PIECE:, :]
+    for member in range(1, RING):
+        packed += parts_ref[member, PIECE:, :]
     gram = jnp.concatenate([packed[:, RANK * a : RANK * (a + 1)] for a in range(4)], axis=0)
     row = lax.broadcasted_iota(jnp.int32, (RANK, RANK), 0)
     column = lax.broadcasted_iota(jnp.int32, (RANK, RANK), 1)
@@ -220,40 +240,51 @@
     return lax.dynamic_index_in_dim(values, at, keepdims=False)
 
 
+def exchange(values, groups):
+    return lax.all_to_all(values, AXES, 0, 0, axis_index_groups=groups)
+
+
+def spread(value, groups):
+    return exchange(jnp.broadcast_to(value[None], (len(groups[0]),) + value.shape), groups)
+
+
+def both_cores(value):
+    return lax.all_gather(value, AXES, axis_index_groups=CHIP_GROUPS)
+
+
 def per_device(grad, error, q_prev):
-    replicas = lax.axis_size(DP)
-    core = lax.axis_index("core").astype(jnp.uint32)
-    mine = (lax.broadcasted_iota(jnp.int32, (8, LANES), 0) == lax.axis_index(Y)).astype(F32)
+    replicas = lax.axis_size("dp")
+    dp = lax.axis_index("dp").astype(jnp.uint32)
+    core = dp % 2
+    row = lax.broadcasted_iota(jnp.uint32, (16, LANES), 0)
+    place = jnp.where(row < 8, row == dp // 2, core == 1).astype(F32)
 
     p_local, merged = left_product(grad[0], error[0], q_prev.T)
-    p_both, mine, core, other = lax.optimization_barrier((lax.all_gather(p_local, "core"), mine, core, 1 - core))
-    p_chip = jnp.sum(p_both, axis=0)
-    p_parts = lax.all_to_all(jnp.broadcast_to(p_chip[None], (NY, RANK, ROWS)), Y_FAR_FIRST, 0, 0)
-
-    pieces, p_sum = right_product(mine, p_parts, merged)
-    traded = lax.all_gather(pick(pieces, other), "core")
-    pieces = pick(pieces, core) + pick(traded, other)
-    pieces = lax.all_to_all(pieces, PLANE, 0, 0)
-    lines = vmem_call(plane_body, in_vmem(NZ, PIECE + 8, LANES))(pieces)
-    lines = lax.all_to_all(lines, Z_FAR_FIRST, 0, 0)
-    own = vmem_call(line_body, in_vmem(NY * NX, PIECE, LANES))(lines)
-    own = lax.all_to_all(own, PLANE, 0, 0)
+    p_both, place, core, other = lax.optimization_barrier((both_cores(p_local), place, core, 1 - core))
+    p_parts = spread(jnp.sum(p_both, axis=0), Y_GROUPS)
+
+    pieces, p_sum = right_product(place, p_parts, merged)
+    traded = both_cores(pick(pieces, other))
+    pieces = exchange(pick(pieces, core) + pick(traded, other), PLANE_GROUPS)
+    lines = vmem_call(plane_body, in_vmem(RING, PIECE + 8, LANES))(place, pieces)
+    lines = exchange(lines, LINE_GROUPS)
+    own = vmem_call(line_body, in_vmem(PLANE, PIECE, LANES))(lines)
+    own = exchange(own, PLANE_GROUPS)
     basis, basis_stack, inverse_stack = vmem_call(
         functools.partial(factor_body, replicas),
         (shape(RANK, ROWS), in_vmem(ROWS, 6 * RANK, dtype=BF16), in_vmem(RANK, 6 * RANK, dtype=BF16)),
     )(lines, p_sum)
-    whole = lax.all_gather(own, "core")
+    whole = both_cores(own)
     new_error, q_new = final(whole, inverse_stack, basis_stack, merged)
     return (new_error[None], basis.T, q_new.T)
 
 
 def solution(mesh):
-    fine = Mesh(mesh.devices.reshape(2, 2, 2, 2, 2, 2, 2, NX), DP + VOCAB)
-    placed = (P(DP, VOCAB, None), P(DP, VOCAB, None), P())
+    placed = (P("dp", "vocab", None), P("dp", "vocab", None), P())
     return jax.shard_map(
         per_device,
-        mesh=fine,
+        mesh=mesh,
         in_specs=placed,
-        out_specs=(P(DP, VOCAB, None), P(VOCAB, None), P()),
+        out_specs=(P("dp", "vocab", None), P("vocab", None), P()),
         check_vma=False,
     )

time: 82.6 us -> 80.4 us (0.973)
  blocking collectives: 60.1 us -> 58.7 us
    all_to_all x3, blocking collectives: 41.9 us -> 40.7 us  [exchange(): return lax.all_to_all(values, AXES, 0, 0, axis_index_groups=groups)]
where the time goes in v5:
time: 80.4 us; the launch traced here: 80.1 us
  blocking collectives  58.7 us (73%)
  Pallas kernels  9.71 us (12%)
  waiting for transfers between devices  6.99 us (9%)
  starting transfers between devices  3.87 us (5%)
    all_to_all x3, blocking collectives, exchange(): return lax.all_to_all(values, AXES, 0, 0, axis_index_groups=groups)  40.7 us
    all_gather x3, blocking collectives, both_cores(): return lax.all_gather(value, AXES, axis_index_groups=CHIP_GROUPS)  17.9 us
    all_to_all x1, waiting for transfers between devices, exchange(): return lax.all_to_all(values, AXES, 0, 0, axis_index_groups=groups)  6.99 us
    pallas_call x4, Pallas kernels, call(): kernel_call(body, out_shape)  5.08 us
    all_to_all x1, starting transfers between devices, exchange(): return lax.all_to_all(values, AXES, 0, 0, axis_index_groups=groups)  3.87 us
    pallas_call x1, Pallas kernels, left_product(): kernel_call(left_body, (in_vmem(RANK, ROWS), in_vmem(ROWS, WIDTH)), in_sp...  2.69 us
    pallas_call x1, Pallas kernels, final(): kernel_call(final_body, (shape(ROWS, WIDTH), shape(RANK, WIDTH)), in_spec...  1.94 us
  transfers between devices with their start and end apart: 1, of which 1 were waited for; matrix products, arithmetic and copies ran while one was open for 0% of the time, Pallas kernels for 4%

profile of v5, /device:TPU:1, one launch (start us, length us, event | category | flops | bytes accessed | tf_op | source)
XLA Modules:
  0.0 80.1 jit_solution(9401779663485050259)
XLA Ops:
  0.6 2.7 %shard_map.58 = (f32[32,128]{1,0:T(8,128)S(1)}, f32[128,3584]{1,0:T(8,128)S(1)}) custom-call(bf16[128,3584]{1,0:T(8,128)(2,1)} %bitcast.12, f32[128,3584]{1,0:T(8,128)} %bitcast.11, f32[32,3584]{1,0:T(8,128)} %bitcast.13), custom_call_target="tpu_custom_call" | custom-call | tf_op jit(solution)/shard_map/pallas_call | solution.py:125
  3.3 8.4 %all-gather = f32[64,128]{1,0:T(8,128)S(1)} all-gather(f32[32,128]{1,0:T(8,128)S(1)} %get-tuple-element.16), channel_id=2, replica_groups={{0,32},{1,33},{2,34},{3,35},{4,36},{5,37},{6,38},{7,39},{8,40},{9,41},{..., dimensions={0}, use_global_device_ids=true | all-gather | bytes 49152 | tf_op jit(solution)/shard_map/all_gather | solution.py:252
  11.7 0.1 iota.10.place_ref
  11.8 9.2 %all_to_all.20.parts_ref = f32[8,32,128]{2,1,0:T(8,128)S(1)} all-to-all(f32[8,32,128]{2,1,0:T(8,128)S(1)} %broadcast_in_dim.14), channel_id=1, replica_groups={{0,256,64,320,128,384,192,448},{1,257,65,321,129,385,193,449},{2,258,66..., dimensions={0} | all-to-all | bytes 262144 | tf_op jit(solution)/shard_map/all_to_all | solution.py:244
  21.0 0.9 %shard_map.59 = (f32[2,32,16,128]{3,2,1,0:T(8,128)S(1)}, f32[32,128]{1,0:T(8,128)S(1)}) custom-call(f32[16,128]{1,0:T(8,128)S(1)} %iota.10.place_ref, f32[8,32,128]{2,1,0:T(8,128)S(1)} %all_to_all.20.parts_ref, f32[128,3584]{1,0:T(8,128)S(1)} %get-tuple-element.19.merged_ref), custom_call_target="tpu_custom_call" | custom-call | tf_op jit(solution)/shard_map/pallas_call | solution.py:83
  21.9 3.5 %all_gather.18 = f32[2,32,16,128]{3,2,1,0:T(8,128)S(1)} all-gather(f32[1,32,16,128]{3,2,1,0:T(8,128)S(1)} %constant_dynamic-slice_fusion), channel_id=1, replica_groups={{0,32},{1,33},{2,34},{3,35},{4,36},{5,37},{6,38},{7,39},{8,40},{9,41},{..., dimensions={0}, use_global_device_ids=true | all-gather | bytes 786432 | tf_op jit(solution)/shard_map/all_gather | solution.py:252
  25.4 22.1 %all_to_all.21.parts_ref = f32[32,16,128]{2,1,0:T(8,128)S(1)} all-to-all(f32[32,16,128]{2,1,0:T(8,128)S(1)} %add_bitcast_fusion), channel_id=1, replica_groups={{0,1,2,3,64,65,66,67,128,129,130,131,192,193,194,195,256,257,258,259,32..., dimensions={0} | all-to-all | bytes 524288 | tf_op jit(solution)/shard_map/all_to_all | solution.py:244
  47.6 9.4 %all_to_all.22.parts_ref = f32[8,24,128]{2,1,0:T(8,128)S(1)} all-to-all(f32[8,24,128]{2,1,0:T(8,128)S(1)} %shard_map.60), channel_id=1, replica_groups={{0,16,4,20,8,24,12,28},{1,17,5,21,9,25,13,29},{2,18,6,22,10,26,14,30},{..., dimensions={0} | all-to-all | bytes 196608 | tf_op jit(solution)/shard_map/all_to_all | solution.py:244
  57.0 0.7 shard_map.61
  57.7 3.9 %all-to-all-start.3 = ((f32[32,16,128]{2,1,0:T(8,128)}), f32[32,16,128]{2,1,0:T(8,128)S(1)}, u32[]{:S(2)}, u32[]{:S(2)}) async-start(f32[32,16,128]{2,1,0:T(8,128)} %shard_map.61), calls=%async_computation.3 | async-start | bytes 524288 | tf_op jit(solution)/shard_map/all_to_all | solution.py:244
  61.6 3.5 %shard_map.62 = (f32[32,128]{1,0:T(8,128)}, bf16[128,192]{1,0:T(8,128)(2,1)S(1)}, bf16[32,192]{1,0:T(8,128)(2,1)S(1)}) custom-call(f32[8,24,128]{2,1,0:T(8,128)S(1)} %all_to_all.22.parts_ref, f32[32,128]{1,0:T(8,128)S(1)} %get-tuple-element.23.p_ref), custom_call_target="tpu_custom_call" | custom-call | tf_op jit(solution)/shard_map/pallas_call | solution.py:83
  65.1 7.0 %all-to-all-done.3 = f32[32,16,128]{2,1,0:T(8,128)S(1)} async-done(((f32[32,16,128]{2,1,0:T(8,128)}), f32[32,16,128]{2,1,0:T(8,128)S(1)}, u32[]{:S(2)}, u32[]{:S(2)}) %all-to-all-start.3) | async-done | bytes 262176 | tf_op jit(solution)/shard_map/all_to_all | solution.py:244
  72.1 6.1 %all-gather.1 = f32[64,16,128]{2,1,0:T(8,128)S(1)} all-gather(f32[32,16,128]{2,1,0:T(8,128)S(1)} %all-to-all-done.3), channel_id=3, replica_groups={{0,32},{1,33},{2,34},{3,35},{4,36},{5,37},{6,38},{7,39},{8,40},{9,41},{..., dimensions={0}, use_global_device_ids=true | all-gather | bytes 786432 | tf_op jit(solution)/shard_map/all_gather | solution.py:252
  78.1 1.9 %shard_map.63 = (f32[128,3584]{1,0:T(8,128)}, f32[32,3584]{1,0:T(8,128)}) custom-call(f32[2,32,16,128]{3,2,1,0:T(8,128)S(1)} %bitcast.10, bf16[32,192]{1,0:T(8,128)(2,1)S(1)} %get-tuple-element.24.inverse_ref, bf16[128,192]{1,0:T(8,128)(2,1)S(1)} %get-tuple-element.25.basis_ref, f32[128,3584]{1,0:T(8,128)S(1)} %get-tuple-element.19.merged_ref), custom_call_target="tpu_custom_call" | custom-call | tf_op jit(solution)/shard_map/pallas_call | solution.py:226
  (6 shorter events, 0.1 us)
Async XLA Ops:
  57.7 14.3 %all-to-all-start.3 = ((f32[32,16,128]{2,1,0:T(8,128)}), f32[32,16,128]{2,1,0:T(8,128)S(1)}, u32[]{:S(2)}, u32[]{:S(2)}) async-start(f32[32,16,128]{2,1,0:T(8,128)} %shard_map.61), calls=%async_computation.3 | async-start | bytes 524288 | tf_op jit(solution)/shard_map/all_to_all | solution.py:244

commit v6 on v5

--- a/solution.py
+++ b/solution.py
@@ -19,22 +19,28 @@
 
 
 FAR_FIRST = (0, 4, 1, 5, 2, 6, 3, 7)
+X_ORDER = (0, 2, 1, 3)
+COST = 10**10
 CHIP_GROUPS = [[device(y, c, z, x) for c in range(2)] for y in range(RING) for z in range(RING) for x in range(NX)]
 Y_GROUPS = [[device(y, c, z, x) for y in FAR_FIRST] for c in range(2) for z in range(RING) for x in range(NX)]
 
 
+CORE_SWAP = [pair for a, b in CHIP_GROUPS for pair in ((a, b), (b, a))]
+
+
 def across(core, a, b, x):
     return device(b, core, a, x) if core else device(a, core, b, x)
 
 
 PLANE_GROUPS = [
-    [across(c, a, b, x) for a in range(RING) for x in range(NX)] for c in range(2) for b in range(RING)
+    [across(c, a, b, x) for x in X_ORDER for a in range(RING)] for c in range(2) for b in range(RING)
 ]
 LINE_GROUPS = [
     [across(c, a, b, x) for b in FAR_FIRST] for c in range(2) for a in range(RING) for x in range(NX)
 ]
 RANK, ROWS, WIDTH = 32, 128, 3584
 HALF = WIDTH // 2
+QUARTER = HALF // 2
 LANES = 128
 TILES = HALF // LANES
 PIECE = TILES + 2
@@ -78,9 +84,9 @@
     )
 
 
-def vmem_call(body, out_shape):
+def vmem_call(body, out_shape, **options):
     def call(*operands):
-        return kernel_call(body, out_shape)(
+        return kernel_call(body, out_shape, **options)(
             *(pltpu.with_memory_space_constraint(value, pltpu.VMEM) for value in operands)
         )
 
@@ -136,35 +142,54 @@
     )(*(pltpu.with_memory_space_constraint(value, pltpu.HBM) for value in (grad, error, q_rows)))
 
 
-def right_body(place_ref, parts_ref, merged_ref, pieces_ref, p_ref):
+def parts_body(place_ref, parts_ref, p_ref, split_ref, row_ref):
     p_sum = jnp.sum(parts_ref[...], axis=0)
     p_ref[...] = p_sum
-    p_parts = jnp.concatenate(split3(p_sum), axis=0)
+    split_ref[...] = jnp.concatenate(split3(p_sum), axis=0)
     gram = lax.dot_general(p_sum, p_sum, NT, precision=HIGHEST, preferred_element_type=F32)
     packed = jnp.concatenate([gram[8 * a : 8 * a + 8] for a in range(4)], axis=1)
-    row = 0.5 * jnp.sum(packed * place_ref[:8, :], axis=0, keepdims=True)
-    for half in range(2):
-        h, m, l = split3(merged_ref[:, half * HALF : (half + 1) * HALF])
+    row = jnp.sum(packed * place_ref[:8, :], axis=0, keepdims=True)
+    row_ref[...] = jnp.broadcast_to(row, (8, LANES))
+
+
+def right_body(split_ref, row_ref, own_ref, taken_ref, pieces_ref, taken_buf, sems):
+    p_parts = split_ref[...]
+    copies = []
+    for at in range(2):
+        columns = pl.ds(at * QUARTER, QUARTER)
+        copies.append(pltpu.make_async_copy(taken_ref.at[:, columns], taken_buf.at[:, columns], sems.at[at]))
+        copies[-1].start()
+    pieces_ref[:, TILES, :] = jnp.broadcast_to(row_ref[:1, :], (RANK, LANES))
+    pieces_ref[:, TILES + 1, :] = jnp.zeros((RANK, LANES), F32)
+    for at in range(2):
+        copies[at].wait()
+        columns = slice(at * QUARTER, (at + 1) * QUARTER)
+        h, m, l = split3(own_ref[:, columns] + taken_buf[:, columns])
         with_h = dot(p_parts, h)
         with_m = dot(p_parts[: 2 * RANK], m)
         with_l = dot(p_parts[:RANK], l)
         small = with_h[2 * RANK :] + with_m[RANK:] + with_l
         product = with_h[:RANK] + (with_h[RANK : 2 * RANK] + with_m[:RANK] + small)
-        for tile in range(TILES):
-            pieces_ref[half, :, tile, :] = product[:, tile * LANES : (tile + 1) * LANES]
-        pieces_ref[half, :, TILES, :] = jnp.broadcast_to(row, (RANK, LANES))
-        pieces_ref[half, :, TILES + 1, :] = jnp.zeros((RANK, LANES), F32)
-
-
-def right_product(place, parts, merged):
-    return vmem_call(right_body, (in_vmem(2, RANK, PIECE, LANES), in_vmem(RANK, ROWS)))(place, parts, merged)
+        for tile in range(TILES // 2):
+            pieces_ref[:, at * (TILES // 2) + tile, :] = product[:, tile * LANES : (tile + 1) * LANES]
+
+
+def right_product(p_split, row, own_half, taken):
+    local = (pltpu.with_memory_space_constraint(value, pltpu.VMEM) for value in (p_split, row, own_half))
+    return kernel_call(
+        right_body,
+        in_vmem(RANK, PIECE, LANES),
+        in_specs=[VMEM] * 3 + [ANY],
+        out_specs=VMEM,
+        scratch_shapes=[pltpu.VMEM((ROWS, HALF), F32), pltpu.SemaphoreType.DMA((2,))],
+    )(*local, taken)
 
 
 def plane_body(place_ref, parts_ref, out_ref):
     rows = parts_ref[0]
     for member in range(1, PLANE):
         rows += parts_ref[member]
-    apart = [sum(parts_ref[a * NX + x, TILES : TILES + 1, :] for x in range(NX)) for a in range(RING)]
+    apart = [sum(parts_ref[x * RING + a, TILES : TILES + 1, :] for x in range(NX)) for a in range(RING)]
     total = apart[FAR_FIRST[0]]
     for z in FAR_FIRST[1:]:
         total += apart[z]
@@ -236,10 +261,6 @@
     )(*(pltpu.with_memory_space_constraint(value, pltpu.VMEM) for value in operands))
 
 
-def pick(values, at):
-    return lax.dynamic_index_in_dim(values, at, keepdims=False)
-
-
 def exchange(values, groups):
     return lax.all_to_all(values, AXES, 0, 0, axis_index_groups=groups)
 
@@ -260,12 +281,17 @@
     place = jnp.where(row < 8, row == dp // 2, core == 1).astype(F32)
 
     p_local, merged = left_product(grad[0], error[0], q_prev.T)
-    p_both, place, core, other = lax.optimization_barrier((both_cores(p_local), place, core, 1 - core))
+    p_both, halves, core = lax.optimization_barrier((both_cores(p_local), merged, core))
+    given = lax.dynamic_slice_in_dim(halves, (1 - core) * HALF, HALF, axis=1)
+    own_half = lax.dynamic_slice_in_dim(halves, core * HALF, HALF, axis=1)
+    taken = lax.ppermute(given, AXES, CORE_SWAP)
     p_parts = spread(jnp.sum(p_both, axis=0), Y_GROUPS)
-
-    pieces, p_sum = right_product(place, p_parts, merged)
-    traded = both_cores(pick(pieces, other))
-    pieces = exchange(pick(pieces, core) + pick(traded, other), PLANE_GROUPS)
+    p_sum, p_split, row = vmem_call(
+        parts_body,
+        (in_vmem(RANK, ROWS), in_vmem(3 * RANK, ROWS, dtype=BF16), in_vmem(8, LANES)),
+        cost_estimate=pl.CostEstimate(flops=COST, bytes_accessed=COST, transcendentals=0),
+    )(place, p_parts)
+    pieces = exchange(right_product(p_split, row, own_half, taken), PLANE_GROUPS)
     lines = vmem_call(plane_body, in_vmem(RING, PIECE + 8, LANES))(place, pieces)
     lines = exchange(lines, LINE_GROUPS)
     own = vmem_call(line_body, in_vmem(PLANE, PIECE, LANES))(lines)

time: 80.4 us -> 81.1 us (level)
  blocking collectives: 58.7 us -> 47.7 us
  starting transfers between devices: 3.87 us -> 9.73 us
  waiting for transfers between devices: 6.99 us -> 9.97 us
  local copies, waits for them, and re-layouts: 0.11 us -> 1.78 us
  Pallas kernels: 9.71 us -> 10.8 us
    all_to_all x3 -> x2, blocking collectives: 40.7 us -> 33.1 us  [exchange(): return lax.all_to_all(values, AXES, 0, 0, axis_index_groups=groups)]
    all_to_all x1 -> x2, starting transfers between devices: 3.87 us -> 7.49 us  [exchange(): return lax.all_to_all(values, AXES, 0, 0, axis_index_groups=groups)]
    all_gather x3 -> x2, blocking collectives: 17.9 us -> 14.6 us  [both_cores(): return lax.all_gather(value, AXES, axis_index_groups=CHIP_GROUPS)]
    all_to_all x1 -> x2, waiting for transfers between devices: 6.99 us -> 9.96 us  [exchange(): return lax.all_to_all(values, AXES, 0, 0, axis_index_groups=groups)]
    ppermute x0 -> x1, starting transfers between devices: none -> 2.24 us  [per_device(): taken = lax.ppermute(given, AXES, CORE_SWAP)]
    pallas_call x4 -> x5, Pallas kernels: 5.08 us -> 6.15 us  [the longest x4 4.44 us: call(): kernel_call(body, out_shape, **options)]
    dynamic_slice x1, local copies, waits for them, and re-layouts: 0.03 us -> 1.05 us  [per_device(): given = lax.dynamic_slice_in_dim(halves, (1 - core) * HALF, HALF, axis=1)]
  transfers between devices with their start and end apart: 1 -> 3, of which waited for: 1 -> 2; matrix products, arithmetic and copies ran while one was open for 0% -> 1% of each run, Pallas kernels for 4% -> 5%
where the time goes in v6:
time: 81.1 us; the launch traced here: 80.7 us
  blocking collectives  47.7 us (59%)
  Pallas kernels  10.8 us (13%)
  waiting for transfers between devices  9.97 us (12%)
  starting transfers between devices  9.73 us (12%)
  local copies, waits for them, and re-layouts  1.78 us (2%)
    all_to_all x2, blocking collectives, exchange(): return lax.all_to_all(values, AXES, 0, 0, axis_index_groups=groups)  33.1 us
    all_gather x2, blocking collectives, both_cores(): return lax.all_gather(value, AXES, axis_index_groups=CHIP_GROUPS)  14.6 us
    all_to_all x2, waiting for transfers between devices, exchange(): return lax.all_to_all(values, AXES, 0, 0, axis_index_groups=groups)  9.96 us
    all_to_all x2, starting transfers between devices, exchange(): return lax.all_to_all(values, AXES, 0, 0, axis_index_groups=groups)  7.49 us
    pallas_call x4, Pallas kernels, call(): kernel_call(body, out_shape, **options)  4.44 us
    pallas_call x1, Pallas kernels, left_product(): kernel_call(left_body, (in_vmem(RANK, ROWS), in_vmem(ROWS, WIDTH)), in_sp...  2.69 us
    ppermute x1, starting transfers between devices, per_device(): taken = lax.ppermute(given, AXES, CORE_SWAP)  2.24 us
    pallas_call x1, Pallas kernels, final(): kernel_call(final_body, (shape(ROWS, WIDTH), shape(RANK, WIDTH)), in_spec...  1.93 us
  transfers between devices with their start and end apart: 3, of which 2 were waited for; matrix products, arithmetic and copies ran while one was open for 1% of the time, Pallas kernels for 5%

profile of v6, /device:TPU:1, one launch (start us, length us, event | category | flops | bytes accessed | tf_op | source)
XLA Modules:
  0.0 80.7 jit_solution(12130098662012165535)
XLA Ops:
  0.6 2.7 %shard_map.58 = (f32[32,128]{1,0:T(8,128)S(1)}, f32[128,3584]{1,0:T(8,128)S(1)}) custom-call(bf16[128,3584]{1,0:T(8,128)(2,1)} %bitcast.10, f32[128,3584]{1,0:T(8,128)} %bitcast.9, f32[32,3584]{1,0:T(8,128)} %bitcast.11), custom_call_target="tpu_custom_call" | custom-call | tf_op jit(solution)/shard_map/pallas_call | solution.py:131
  3.3 8.4 %all-gather = f32[64,128]{1,0:T(8,128)S(1)} all-gather(f32[32,128]{1,0:T(8,128)S(1)} %get-tuple-element.16), channel_id=2, replica_groups={{0,32},{1,33},{2,34},{3,35},{4,36},{5,37},{6,38},{7,39},{8,40},{9,41},{..., dimensions={0}, use_global_device_ids=true | all-gather | bytes 49152 | tf_op jit(solution)/shard_map/all_gather | solution.py:273
  11.7 0.7 broadcast_in_dim.14
  12.4 3.4 %all-to-all-start = ((f32[8,32,128]{2,1,0:T(8,128)}), f32[8,32,128]{2,1,0:T(8,128)S(1)}, u32[]{:S(2)}, u32[]{:S(2)}) async-start(f32[8,32,128]{2,1,0:T(8,128)} %broadcast_in_dim.14), calls=%async_computation | async-start | bytes 262144 | tf_op jit(solution)/shard_map/all_to_all | solution.py:265
  15.8 1.0 %constant_dynamic-slice_fusion = (f32[128,1792]{1,0:T(8,128)}, f32[128,1792]{1,0:T(8,128)S(1)}) fusion(f32[128,3584]{1,0:T(8,128)S(1)} %get-tuple-element.21.merged_ref, u32[]{:T(128)S(6)} %mul.7, u32[]{:T(128)S(6)} %mul.6), kind=kLoop, calls=%fused_computation.1 | loop fusion | bytes 3670024 | tf_op jit(solution)/shard_map/dynamic_slice | solution.py:285
  16.8 2.2 %collective-permute-start = (f32[128,1792]{1,0:T(8,128)}, f32[128,1792]{1,0:T(8,128)}, u32[]{:S(2)}, u32[]{:S(2)}) collective-permute-start(f32[128,1792]{1,0:T(8,128)} %get-tuple-element.29), channel_id=1, source_target_pairs={{0,32},{32,0},{1,33},{33,1},{2,34},{34,2},{3,35},{35,3},{4,36},{36... | collective-permute-start | bytes 2752520 | tf_op jit(solution)/shard_map/ppermute | solution.py:287
  19.1 3.4 %all-to-all-done.parts_ref = f32[8,32,128]{2,1,0:T(8,128)S(1)} async-done(((f32[8,32,128]{2,1,0:T(8,128)}), f32[8,32,128]{2,1,0:T(8,128)S(1)}, u32[]{:S(2)}, u32[]{:S(2)}) %all-to-all-start) | async-done | bytes 131104 | tf_op jit(solution)/shard_map/all_to_all | solution.py:265
  22.5 0.1 iota.10.place_ref
  22.5 0.2 shard_map.59
  22.8 0.0 collective-permute-done.taken_ref
  22.8 1.7 %shard_map.60 = f32[32,16,128]{2,1,0:T(8,128)S(1)} custom-call(bf16[96,128]{1,0:T(8,128)(2,1)S(1)} %get-tuple-element.19.split_ref, f32[8,128]{1,0:T(8,128)S(1)} %get-tuple-element.20.row_ref, f32[128,1792]{1,0:T(8,128)S(1)} %get-tuple-element.30.own_ref, f32[128,1792]{1,0:T(8,128)} %collective-permute-done.taken_ref), custom_call_target="tpu_custom_call" | custom-call | tf_op jit(solution)/shard_map/pallas_call | solution.py:179
  24.5 20.8 %all_to_all.20.parts_ref = f32[32,16,128]{2,1,0:T(8,128)S(1)} all-to-all(f32[32,16,128]{2,1,0:T(8,128)S(1)} %shard_map.60), channel_id=1, replica_groups={{0,64,128,192,256,320,384,448,2,66,130,194,258,322,386,450,1,65,129,193..., dimensions={0} | all-to-all | bytes 524288 | tf_op jit(solution)/shard_map/all_to_all | solution.py:265
  45.3 12.3 %all_to_all.21.parts_ref = f32[8,24,128]{2,1,0:T(8,128)S(1)} all-to-all(f32[8,24,128]{2,1,0:T(8,128)S(1)} %shard_map.61), channel_id=1, replica_groups={{0,16,4,20,8,24,12,28},{1,17,5,21,9,25,13,29},{2,18,6,22,10,26,14,30},{..., dimensions={0} | all-to-all | bytes 196608 | tf_op jit(solution)/shard_map/all_to_all | solution.py:265
  57.6 0.7 shard_map.62
  58.4 4.1 %all-to-all-start.3 = ((f32[32,16,128]{2,1,0:T(8,128)}), f32[32,16,128]{2,1,0:T(8,128)S(1)}, u32[]{:S(2)}, u32[]{:S(2)}) async-start(f32[32,16,128]{2,1,0:T(8,128)} %shard_map.62), calls=%async_computation.3 | async-start | bytes 524288 | tf_op jit(solution)/shard_map/all_to_all | solution.py:265
  62.5 3.5 %shard_map.63 = (f32[32,128]{1,0:T(8,128)}, bf16[128,192]{1,0:T(8,128)(2,1)S(1)}, bf16[32,192]{1,0:T(8,128)(2,1)S(1)}) custom-call(f32[8,24,128]{2,1,0:T(8,128)S(1)} %all_to_all.21.parts_ref, f32[32,128]{1,0:T(8,128)S(1)} %get-tuple-element.23.p_ref), custom_call_target="tpu_custom_call" | custom-call | tf_op jit(solution)/shard_map/pallas_call | solution.py:89
  65.9 6.6 %all-to-all-done.3 = f32[32,16,128]{2,1,0:T(8,128)S(1)} async-done(((f32[32,16,128]{2,1,0:T(8,128)}), f32[32,16,128]{2,1,0:T(8,128)S(1)}, u32[]{:S(2)}, u32[]{:S(2)}) %all-to-all-start.3) | async-done | bytes 262176 | tf_op jit(solution)/shard_map/all_to_all | solution.py:265
  72.5 6.2 %all-gather.1 = f32[64,16,128]{2,1,0:T(8,128)S(1)} all-gather(f32[32,16,128]{2,1,0:T(8,128)S(1)} %all-to-all-done.3), channel_id=3, replica_groups={{0,32},{1,33},{2,34},{3,35},{4,36},{5,37},{6,38},{7,39},{8,40},{9,41},{..., dimensions={0}, use_global_device_ids=true | all-gather | bytes 786432 | tf_op jit(solution)/shard_map/all_gather | solution.py:273
  78.7 1.9 %shard_map.64 = (f32[128,3584]{1,0:T(8,128)}, f32[32,3584]{1,0:T(8,128)}) custom-call(f32[2,32,16,128]{3,2,1,0:T(8,128)S(1)} %bitcast.8, bf16[32,192]{1,0:T(8,128)(2,1)S(1)} %get-tuple-element.24.inverse_ref, bf16[128,192]{1,0:T(8,128)(2,1)S(1)} %get-tuple-element.25.basis_ref, f32[128,3584]{1,0:T(8,128)S(1)} %get-tuple-element.21.merged_ref), custom_call_target="tpu_custom_call" | custom-call | tf_op jit(solution)/shard_map/pallas_call | solution.py:251
  (3 shorter events, 0.0 us)
Async XLA Ops:
  12.4 10.1 %all-to-all-start = ((f32[8,32,128]{2,1,0:T(8,128)}), f32[8,32,128]{2,1,0:T(8,128)S(1)}, u32[]{:S(2)}, u32[]{:S(2)}) async-start(f32[8,32,128]{2,1,0:T(8,128)} %broadcast_in_dim.14), calls=%async_computation | async-start | bytes 262144 | tf_op jit(solution)/shard_map/all_to_all | solution.py:265
  16.8 6.0 %collective-permute-start = (f32[128,1792]{1,0:T(8,128)}, f32[128,1792]{1,0:T(8,128)}, u32[]{:S(2)}, u32[]{:S(2)}) collective-permute-start(f32[128,1792]{1,0:T(8,128)} %get-tuple-element.29), channel_id=1, source_target_pairs={{0,32},{32,0},{1,33},{33,1},{2,34},{34,2},{3,35},{35,3},{4,36},{36... | collective-permute-start | bytes 2752520 | tf_op jit(solution)/shard_map/ppermute | solution.py:287
  58.4 14.2 %all-to-all-start.3 = ((f32[32,16,128]{2,1,0:T(8,128)}), f32[32,16,128]{2,1,0:T(8,128)S(1)}, u32[]{:S(2)}, u32[]{:S(2)}) async-start(f32[32,16,128]{2,1,0:T(8,128)} %shard_map.62), calls=%async_computation.3 | async-start | bytes 524288 | tf_op jit(solution)/shard_map/all_to_all | solution.py:265

commit v7 on v5

--- a/solution.py
+++ b/solution.py
@@ -19,16 +19,17 @@
 
 
 FAR_FIRST = (0, 4, 1, 5, 2, 6, 3, 7)
+X_ORDER = (0, 2, 1, 3)
 CHIP_GROUPS = [[device(y, c, z, x) for c in range(2)] for y in range(RING) for z in range(RING) for x in range(NX)]
 Y_GROUPS = [[device(y, c, z, x) for y in FAR_FIRST] for c in range(2) for z in range(RING) for x in range(NX)]
 
 
 def across(core, a, b, x):
-    return device(b, core, a, x) if core else device(a, core, b, x)
+    return device(a, core, b, x) if core else device(b, core, a, x)
 
 
 PLANE_GROUPS = [
-    [across(c, a, b, x) for a in range(RING) for x in range(NX)] for c in range(2) for b in range(RING)
+    [across(c, a, b, x) for x in X_ORDER for a in range(RING)] for c in range(2) for b in range(RING)
 ]
 LINE_GROUPS = [
     [across(c, a, b, x) for b in FAR_FIRST] for c in range(2) for a in range(RING) for x in range(NX)
@@ -164,7 +165,7 @@
     rows = parts_ref[0]
     for member in range(1, PLANE):
         rows += parts_ref[member]
-    apart = [sum(parts_ref[a * NX + x, TILES : TILES + 1, :] for x in range(NX)) for a in range(RING)]
+    apart = [sum(parts_ref[x * RING + a, TILES : TILES + 1, :] for x in range(NX)) for a in range(RING)]
     total = apart[FAR_FIRST[0]]
     for z in FAR_FIRST[1:]:
         total += apart[z]
@@ -257,7 +258,7 @@
     dp = lax.axis_index("dp").astype(jnp.uint32)
     core = dp % 2
     row = lax.broadcasted_iota(jnp.uint32, (16, LANES), 0)
-    place = jnp.where(row < 8, row == dp // 2, core == 1).astype(F32)
+    place = jnp.where(row < 8, row == dp // 2, core == 0).astype(F32)
 
     p_local, merged = left_product(grad[0], error[0], q_prev.T)
     p_both, place, core, other = lax.optimization_barrier((both_cores(p_local), place, core, 1 - core))

time: 80.4 us -> 80 us (level)
  no operation moved by 1% of the time
where the time goes in v7:
time: 80 us; the launch traced here: 79.6 us
  blocking collectives  58.3 us (73%)
  Pallas kernels  9.72 us (12%)
  waiting for transfers between devices  6.59 us (8%)
  starting transfers between devices  4.13 us (5%)
    all_to_all x3, blocking collectives, exchange(): return lax.all_to_all(values, AXES, 0, 0, axis_index_groups=groups)  40.4 us
    all_gather x3, blocking collectives, both_cores(): return lax.all_gather(value, AXES, axis_index_groups=CHIP_GROUPS)  17.9 us
    all_to_all x1, waiting for transfers between devices, exchange(): return lax.all_to_all(values, AXES, 0, 0, axis_index_groups=groups)  6.59 us
    pallas_call x4, Pallas kernels, call(): kernel_call(body, out_shape)  5.09 us
    all_to_all x1, starting transfers between devices, exchange(): return lax.all_to_all(values, AXES, 0, 0, axis_index_groups=groups)  4.13 us
    pallas_call x1, Pallas kernels, left_product(): kernel_call(left_body, (in_vmem(RANK, ROWS), in_vmem(ROWS, WIDTH)), in_sp...  2.69 us
    pallas_call x1, Pallas kernels, final(): kernel_call(final_body, (shape(ROWS, WIDTH), shape(RANK, WIDTH)), in_spec...  1.94 us
  transfers between devices with their start and end apart: 1, of which 1 were waited for; matrix products, arithmetic and copies ran while one was open for 0% of the time, Pallas kernels for 4%

profile of v7, /device:TPU:1, one launch (start us, length us, event | category | flops | bytes accessed | tf_op | source)
XLA Modules:
  0.0 79.6 jit_solution(14852157519949217617)
XLA Ops:
  0.6 2.7 %shard_map.58 = (f32[32,128]{1,0:T(8,128)S(1)}, f32[128,3584]{1,0:T(8,128)S(1)}) custom-call(bf16[128,3584]{1,0:T(8,128)(2,1)} %bitcast.12, f32[128,3584]{1,0:T(8,128)} %bitcast.11, f32[32,3584]{1,0:T(8,128)} %bitcast.13), custom_call_target="tpu_custom_call" | custom-call | tf_op jit(solution)/shard_map/pallas_call | solution.py:126
  3.3 8.4 %all-gather = f32[64,128]{1,0:T(8,128)S(1)} all-gather(f32[32,128]{1,0:T(8,128)S(1)} %get-tuple-element.16), channel_id=2, replica_groups={{0,32},{1,33},{2,34},{3,35},{4,36},{5,37},{6,38},{7,39},{8,40},{9,41},{..., dimensions={0}, use_global_device_ids=true | all-gather | bytes 49152 | tf_op jit(solution)/shard_map/all_gather | solution.py:253
  11.7 0.1 iota.10.place_ref
  11.8 9.2 %all_to_all.20.parts_ref = f32[8,32,128]{2,1,0:T(8,128)S(1)} all-to-all(f32[8,32,128]{2,1,0:T(8,128)S(1)} %broadcast_in_dim.14), channel_id=1, replica_groups={{0,256,64,320,128,384,192,448},{1,257,65,321,129,385,193,449},{2,258,66..., dimensions={0} | all-to-all | bytes 262144 | tf_op jit(solution)/shard_map/all_to_all | solution.py:245
  21.0 0.9 %shard_map.59 = (f32[2,32,16,128]{3,2,1,0:T(8,128)S(1)}, f32[32,128]{1,0:T(8,128)S(1)}) custom-call(f32[16,128]{1,0:T(8,128)S(1)} %iota.10.place_ref, f32[8,32,128]{2,1,0:T(8,128)S(1)} %all_to_all.20.parts_ref, f32[128,3584]{1,0:T(8,128)S(1)} %get-tuple-element.19.merged_ref), custom_call_target="tpu_custom_call" | custom-call | tf_op jit(solution)/shard_map/pallas_call | solution.py:84
  21.9 3.5 %all_gather.18 = f32[2,32,16,128]{3,2,1,0:T(8,128)S(1)} all-gather(f32[1,32,16,128]{3,2,1,0:T(8,128)S(1)} %constant_dynamic-slice_fusion), channel_id=1, replica_groups={{0,32},{1,33},{2,34},{3,35},{4,36},{5,37},{6,38},{7,39},{8,40},{9,41},{..., dimensions={0}, use_global_device_ids=true | all-gather | bytes 786432 | tf_op jit(solution)/shard_map/all_gather | solution.py:253
  25.4 14.6 %all_to_all.21.parts_ref = f32[32,16,128]{2,1,0:T(8,128)S(1)} all-to-all(f32[32,16,128]{2,1,0:T(8,128)S(1)} %add_bitcast_fusion), channel_id=1, replica_groups={{0,4,8,12,16,20,24,28,2,6,10,14,18,22,26,30,1,5,9,13,17,21,25,29,3,7,11..., dimensions={0} | all-to-all | bytes 524288 | tf_op jit(solution)/shard_map/all_to_all | solution.py:245
  40.1 16.6 %all_to_all.22.parts_ref = f32[8,24,128]{2,1,0:T(8,128)S(1)} all-to-all(f32[8,24,128]{2,1,0:T(8,128)S(1)} %shard_map.60), channel_id=1, replica_groups={{0,256,64,320,128,384,192,448},{1,257,65,321,129,385,193,449},{2,258,66..., dimensions={0} | all-to-all | bytes 196608 | tf_op jit(solution)/shard_map/all_to_all | solution.py:245
  56.7 0.7 shard_map.61
  57.4 4.1 %all-to-all-start.3 = ((f32[32,16,128]{2,1,0:T(8,128)}), f32[32,16,128]{2,1,0:T(8,128)S(1)}, u32[]{:S(2)}, u32[]{:S(2)}) async-start(f32[32,16,128]{2,1,0:T(8,128)} %shard_map.61), calls=%async_computation.3 | async-start | bytes 524288 | tf_op jit(solution)/shard_map/all_to_all | solution.py:245
  61.5 3.5 %shard_map.62 = (f32[32,128]{1,0:T(8,128)}, bf16[128,192]{1,0:T(8,128)(2,1)S(1)}, bf16[32,192]{1,0:T(8,128)(2,1)S(1)}) custom-call(f32[8,24,128]{2,1,0:T(8,128)S(1)} %all_to_all.22.parts_ref, f32[32,128]{1,0:T(8,128)S(1)} %get-tuple-element.23.p_ref), custom_call_target="tpu_custom_call" | custom-call | tf_op jit(solution)/shard_map/pallas_call | solution.py:84
  65.0 6.6 %all-to-all-done.3 = f32[32,16,128]{2,1,0:T(8,128)S(1)} async-done(((f32[32,16,128]{2,1,0:T(8,128)}), f32[32,16,128]{2,1,0:T(8,128)S(1)}, u32[]{:S(2)}, u32[]{:S(2)}) %all-to-all-start.3) | async-done | bytes 262176 | tf_op jit(solution)/shard_map/all_to_all | solution.py:245
  71.6 6.1 %all-gather.1 = f32[64,16,128]{2,1,0:T(8,128)S(1)} all-gather(f32[32,16,128]{2,1,0:T(8,128)S(1)} %all-to-all-done.3), channel_id=3, replica_groups={{0,32},{1,33},{2,34},{3,35},{4,36},{5,37},{6,38},{7,39},{8,40},{9,41},{..., dimensions={0}, use_global_device_ids=true | all-gather | bytes 786432 | tf_op jit(solution)/shard_map/all_gather | solution.py:253
  77.7 1.9 %shard_map.63 = (f32[128,3584]{1,0:T(8,128)}, f32[32,3584]{1,0:T(8,128)}) custom-call(f32[2,32,16,128]{3,2,1,0:T(8,128)S(1)} %bitcast.10, bf16[32,192]{1,0:T(8,128)(2,1)S(1)} %get-tuple-element.24.inverse_ref, bf16[128,192]{1,0:T(8,128)(2,1)S(1)} %get-tuple-element.25.basis_ref, f32[128,3584]{1,0:T(8,128)S(1)} %get-tuple-element.19.merged_ref), custom_call_target="tpu_custom_call" | custom-call | tf_op jit(solution)/shard_map/pallas_call | solution.py:227
  (6 shorter events, 0.1 us)
Async XLA Ops:
  57.4 14.2 %all-to-all-start.3 = ((f32[32,16,128]{2,1,0:T(8,128)}), f32[32,16,128]{2,1,0:T(8,128)S(1)}, u32[]{:S(2)}, u32[]{:S(2)}) async-start(f32[32,16,128]{2,1,0:T(8,128)} %shard_map.61), calls=%async_computation.3 | async-start | bytes 524288 | tf_op jit(solution)/shard_map/all_to_all | solution.py:245

commit v8 on v7

--- a/solution.py
+++ b/solution.py
@@ -137,13 +137,25 @@
     )(*(pltpu.with_memory_space_constraint(value, pltpu.HBM) for value in (grad, error, q_rows)))
 
 
-def right_body(place_ref, parts_ref, merged_ref, pieces_ref, p_ref):
+def one_row(rows):
+    return (lax.broadcasted_iota(jnp.int32, (rows, LANES), 0) == lax.axis_index("dp") // 2).astype(F32)
+
+
+def right_body(parts_ref, merged_ref, own_ref, given_ref, p_ref):
+    core = lax.axis_index("dp") % 2
     p_sum = jnp.sum(parts_ref[...], axis=0)
     p_ref[...] = p_sum
     p_parts = jnp.concatenate(split3(p_sum), axis=0)
     gram = lax.dot_general(p_sum, p_sum, NT, precision=HIGHEST, preferred_element_type=F32)
     packed = jnp.concatenate([gram[8 * a : 8 * a + 8] for a in range(4)], axis=1)
-    row = 0.5 * jnp.sum(packed * place_ref[:8, :], axis=0, keepdims=True)
+    row = jnp.broadcast_to(0.5 * jnp.sum(packed * one_row(8), axis=0, keepdims=True), (RANK, LANES))
+
+    def store(ref, product):
+        for tile in range(TILES):
+            ref[:, tile, :] = product[:, tile * LANES : (tile + 1) * LANES]
+        ref[:, TILES, :] = row
+        ref[:, TILES + 1, :] = jnp.zeros((RANK, LANES), F32)
+
     for half in range(2):
         h, m, l = split3(merged_ref[:, half * HALF : (half + 1) * HALF])
         with_h = dot(p_parts, h)
@@ -151,17 +163,16 @@
         with_l = dot(p_parts[:RANK], l)
         small = with_h[2 * RANK :] + with_m[RANK:] + with_l
         product = with_h[:RANK] + (with_h[RANK : 2 * RANK] + with_m[:RANK] + small)
-        for tile in range(TILES):
-            pieces_ref[half, :, tile, :] = product[:, tile * LANES : (tile + 1) * LANES]
-        pieces_ref[half, :, TILES, :] = jnp.broadcast_to(row, (RANK, LANES))
-        pieces_ref[half, :, TILES + 1, :] = jnp.zeros((RANK, LANES), F32)
-
-
-def right_product(place, parts, merged):
-    return vmem_call(right_body, (in_vmem(2, RANK, PIECE, LANES), in_vmem(RANK, ROWS)))(place, parts, merged)
-
-
-def plane_body(place_ref, parts_ref, out_ref):
+        pl.when(core == half)(functools.partial(store, own_ref, product))
+        pl.when(core != half)(functools.partial(store, given_ref, product))
+
+
+def right_product(parts, merged):
+    pieces = in_vmem(RANK, PIECE, LANES)
+    return vmem_call(right_body, (pieces, pieces, in_vmem(RANK, ROWS)))(parts, merged)
+
+
+def plane_body(parts_ref, out_ref):
     rows = parts_ref[0]
     for member in range(1, PLANE):
         rows += parts_ref[member]
@@ -169,7 +180,7 @@
     total = apart[FAR_FIRST[0]]
     for z in FAR_FIRST[1:]:
         total += apart[z]
-    gram = jnp.where(place_ref[8:, :] > 0, total * place_ref[:8, :], jnp.concatenate(apart, axis=0))
+    gram = jnp.where(lax.axis_index("dp") % 2 == 0, total * one_row(8), jnp.concatenate(apart, axis=0))
     both = jnp.concatenate([rows, gram], axis=0)
     for member in range(RING):
         out_ref[member] = both
@@ -237,10 +248,6 @@
     )(*(pltpu.with_memory_space_constraint(value, pltpu.VMEM) for value in operands))
 
 
-def pick(values, at):
-    return lax.dynamic_index_in_dim(values, at, keepdims=False)
-
-
 def exchange(values, groups):
     return lax.all_to_all(values, AXES, 0, 0, axis_index_groups=groups)
 
@@ -255,19 +262,16 @@
 
 def per_device(grad, error, q_prev):
     replicas = lax.axis_size("dp")
-    dp = lax.axis_index("dp").astype(jnp.uint32)
-    core = dp % 2
-    row = lax.broadcasted_iota(jnp.uint32, (16, LANES), 0)
-    place = jnp.where(row < 8, row == dp // 2, core == 0).astype(F32)
+    other = 1 - lax.axis_index("dp").astype(jnp.uint32) % 2
 
     p_local, merged = left_product(grad[0], error[0], q_prev.T)
-    p_both, place, core, other = lax.optimization_barrier((both_cores(p_local), place, core, 1 - core))
+    p_both, other = lax.optimization_barrier((both_cores(p_local), other))
     p_parts = spread(jnp.sum(p_both, axis=0), Y_GROUPS)
 
-    pieces, p_sum = right_product(place, p_parts, merged)
-    traded = both_cores(pick(pieces, other))
-    pieces = exchange(pick(pieces, core) + pick(traded, other), PLANE_GROUPS)
-    lines = vmem_call(plane_body, in_vmem(RING, PIECE + 8, LANES))(place, pieces)
+    pieces, given, p_sum = right_product(p_parts, merged)
+    pieces += lax.dynamic_index_in_dim(both_cores(given), other, keepdims=False)
+    pieces = exchange(pieces, PLANE_GROUPS)
+    lines = vmem_call(plane_body, in_vmem(RING, PIECE + 8, LANES))(pieces)
     lines = exchange(lines, LINE_GROUPS)
     own = vmem_call(line_body, in_vmem(PLANE, PIECE, LANES))(lines)
     own = exchange(own, PLANE_GROUPS)

time: 80 us -> 80 us (level)
  no operation moved by 1% of the time
where the time goes in v8:
time: 80 us; the launch traced here: 79.7 us
  blocking collectives  58.3 us (73%)
  Pallas kernels  9.97 us (12%)
  waiting for transfers between devices  6.58 us (8%)
  starting transfers between devices  4.13 us (5%)
    all_to_all x3, blocking collectives, exchange(): return lax.all_to_all(values, AXES, 0, 0, axis_index_groups=groups)  40.4 us
    all_gather x3, blocking collectives, both_cores(): return lax.all_gather(value, AXES, axis_index_groups=CHIP_GROUPS)  17.9 us
    all_to_all x1, waiting for transfers between devices, exchange(): return lax.all_to_all(values, AXES, 0, 0, axis_index_groups=groups)  6.58 us
    pallas_call x4, Pallas kernels, call(): kernel_call(body, out_shape)  5.34 us
    all_to_all x1, starting transfers between devices, exchange(): return lax.all_to_all(values, AXES, 0, 0, axis_index_groups=groups)  4.13 us
    pallas_call x1, Pallas kernels, left_product(): kernel_call(left_body, (in_vmem(RANK, ROWS), in_vmem(ROWS, WIDTH)), in_sp...  2.69 us
    pallas_call x1, Pallas kernels, final(): kernel_call(final_body, (shape(ROWS, WIDTH), shape(RANK, WIDTH)), in_spec...  1.94 us
  transfers between devices with their start and end apart: 1, of which 1 were waited for; matrix products, arithmetic and copies ran while one was open for 0% of the time, Pallas kernels for 4%

profile of v8, /device:TPU:1, one launch (start us, length us, event | category | flops | bytes accessed | tf_op | source)
XLA Modules:
  0.0 79.7 jit_solution(4849857584778537304)
XLA Ops:
  0.6 2.7 %shard_map.58 = (f32[32,128]{1,0:T(8,128)S(1)}, f32[128,3584]{1,0:T(8,128)S(1)}) custom-call(bf16[128,3584]{1,0:T(8,128)(2,1)} %bitcast.14, f32[128,3584]{1,0:T(8,128)} %bitcast.12, f32[32,3584]{1,0:T(8,128)} %bitcast.15), custom_call_target="tpu_custom_call" | custom-call | tf_op jit(solution)/shard_map/pallas_call | solution.py:126
  3.3 8.4 %all-gather = f32[64,128]{1,0:T(8,128)S(1)} all-gather(f32[32,128]{1,0:T(8,128)S(1)} %get-tuple-element.15), channel_id=2, replica_groups={{0,32},{1,33},{2,34},{3,35},{4,36},{5,37},{6,38},{7,39},{8,40},{9,41},{..., dimensions={0}, use_global_device_ids=true | all-gather | bytes 49152 | tf_op jit(solution)/shard_map/all_gather | solution.py:260
  11.7 9.2 %all_to_all.20.parts_ref = f32[8,32,128]{2,1,0:T(8,128)S(1)} all-to-all(f32[8,32,128]{2,1,0:T(8,128)S(1)} %broadcast_in_dim.4), channel_id=1, replica_groups={{0,256,64,320,128,384,192,448},{1,257,65,321,129,385,193,449},{2,258,66..., dimensions={0} | all-to-all | bytes 262144 | tf_op jit(solution)/shard_map/all_to_all | solution.py:252
  20.9 1.1 %shard_map.59 = (f32[32,16,128]{2,1,0:T(8,128)S(1)}, f32[32,16,128]{2,1,0:T(8,128)S(1)}, f32[32,128]{1,0:T(8,128)S(1)}) custom-call(f32[8,32,128]{2,1,0:T(8,128)S(1)} %all_to_all.20.parts_ref, f32[128,3584]{1,0:T(8,128)S(1)} %get-tuple-element.17.merged_ref), custom_call_target="tpu_custom_call" | custom-call | tf_op jit(solution)/shard_map/pallas_call | solution.py:84
  22.0 3.4 %all-gather.1 = f32[64,16,128]{2,1,0:T(8,128)S(1)} all-gather(f32[32,16,128]{2,1,0:T(8,128)S(1)} %get-tuple-element.19), channel_id=3, replica_groups={{0,32},{1,33},{2,34},{3,35},{4,36},{5,37},{6,38},{7,39},{8,40},{9,41},{..., dimensions={0}, use_global_device_ids=true | all-gather | bytes 786432 | tf_op jit(solution)/shard_map/all_gather | solution.py:260
  25.5 14.6 %all_to_all.21.parts_ref = f32[32,16,128]{2,1,0:T(8,128)S(1)} all-to-all(f32[32,16,128]{2,1,0:T(8,128)S(1)} %bitcast_add_fusion), channel_id=1, replica_groups={{0,4,8,12,16,20,24,28,2,6,10,14,18,22,26,30,1,5,9,13,17,21,25,29,3,7,11..., dimensions={0} | all-to-all | bytes 524288 | tf_op jit(solution)/shard_map/all_to_all | solution.py:252
  40.2 16.6 %all_to_all.22.parts_ref = f32[8,24,128]{2,1,0:T(8,128)S(1)} all-to-all(f32[8,24,128]{2,1,0:T(8,128)S(1)} %shard_map.60), channel_id=1, replica_groups={{0,256,64,320,128,384,192,448},{1,257,65,321,129,385,193,449},{2,258,66..., dimensions={0} | all-to-all | bytes 196608 | tf_op jit(solution)/shard_map/all_to_all | solution.py:252
  56.7 0.7 shard_map.61
  57.5 4.1 %all-to-all-start.3 = ((f32[32,16,128]{2,1,0:T(8,128)}), f32[32,16,128]{2,1,0:T(8,128)S(1)}, u32[]{:S(2)}, u32[]{:S(2)}) async-start(f32[32,16,128]{2,1,0:T(8,128)} %shard_map.61), calls=%async_computation.3 | async-start | bytes 524288 | tf_op jit(solution)/shard_map/all_to_all | solution.py:252
  61.6 3.5 %shard_map.62 = (f32[32,128]{1,0:T(8,128)}, bf16[128,192]{1,0:T(8,128)(2,1)S(1)}, bf16[32,192]{1,0:T(8,128)(2,1)S(1)}) custom-call(f32[8,24,128]{2,1,0:T(8,128)S(1)} %all_to_all.22.parts_ref, f32[32,128]{1,0:T(8,128)S(1)} %get-tuple-element.21.p_ref), custom_call_target="tpu_custom_call" | custom-call | tf_op jit(solution)/shard_map/pallas_call | solution.py:84
  65.1 6.6 %all-to-all-done.3 = f32[32,16,128]{2,1,0:T(8,128)S(1)} async-done(((f32[32,16,128]{2,1,0:T(8,128)}), f32[32,16,128]{2,1,0:T(8,128)S(1)}, u32[]{:S(2)}, u32[]{:S(2)}) %all-to-all-start.3) | async-done | bytes 262176 | tf_op jit(solution)/shard_map/all_to_all | solution.py:252
  71.6 6.1 %all-gather.2 = f32[64,16,128]{2,1,0:T(8,128)S(1)} all-gather(f32[32,16,128]{2,1,0:T(8,128)S(1)} %all-to-all-done.3), channel_id=4, replica_groups={{0,32},{1,33},{2,34},{3,35},{4,36},{5,37},{6,38},{7,39},{8,40},{9,41},{..., dimensions={0}, use_global_device_ids=true | all-gather | bytes 786432 | tf_op jit(solution)/shard_map/all_gather | solution.py:260
  77.8 1.9 %shard_map.63 = (f32[128,3584]{1,0:T(8,128)}, f32[32,3584]{1,0:T(8,128)}) custom-call(f32[2,32,16,128]{3,2,1,0:T(8,128)S(1)} %bitcast.11, bf16[32,192]{1,0:T(8,128)(2,1)S(1)} %get-tuple-element.22.inverse_ref, bf16[128,192]{1,0:T(8,128)(2,1)S(1)} %get-tuple-element.23.basis_ref, f32[128,3584]{1,0:T(8,128)S(1)} %get-tuple-element.17.merged_ref), custom_call_target="tpu_custom_call" | custom-call | tf_op jit(solution)/shard_map/pallas_call | solution.py:238
  (4 shorter events, 0.1 us)
Async XLA Ops:
  57.5 14.2 %all-to-all-start.3 = ((f32[32,16,128]{2,1,0:T(8,128)}), f32[32,16,128]{2,1,0:T(8,128)S(1)}, u32[]{:S(2)}, u32[]{:S(2)}) async-start(f32[32,16,128]{2,1,0:T(8,128)} %shard_map.61), calls=%async_computation.3 | async-start | bytes 524288 | tf_op jit(solution)/shard_map/all_to_all | solution.py:252

commit v9 on v7

--- a/solution.py
+++ b/solution.py
@@ -261,8 +261,8 @@
     place = jnp.where(row < 8, row == dp // 2, core == 0).astype(F32)
 
     p_local, merged = left_product(grad[0], error[0], q_prev.T)
-    p_both, place, core, other = lax.optimization_barrier((both_cores(p_local), place, core, 1 - core))
-    p_parts = spread(jnp.sum(p_both, axis=0), Y_GROUPS)
+    p_local, place, core, other = lax.optimization_barrier((p_local, place, core, 1 - core))
+    p_parts = both_cores(jnp.sum(spread(p_local, Y_GROUPS), axis=0))
 
     pieces, p_sum = right_product(place, p_parts, merged)
     traded = both_cores(pick(pieces, other))

time: 80 us -> 79.8 us (level)
    all_gather x3, blocking collectives: 17.9 us -> 12.6 us  [both_cores(): return lax.all_gather(value, AXES, axis_index_groups=CHIP_GROUPS)]
    all_to_all x3, blocking collectives: 40.4 us -> 45.6 us  [exchange(): return lax.all_to_all(values, AXES, 0, 0, axis_index_groups=groups)]
where the time goes in v9:
time: 79.8 us; the launch traced here: 79.5 us
  blocking collectives  58.2 us (73%)
  Pallas kernels  9.72 us (12%)
  waiting for transfers between devices  6.62 us (8%)
  starting transfers between devices  4.06 us (5%)
    all_to_all x3, blocking collectives, exchange(): return lax.all_to_all(values, AXES, 0, 0, axis_index_groups=groups)  45.6 us
    all_gather x3, blocking collectives, both_cores(): return lax.all_gather(value, AXES, axis_index_groups=CHIP_GROUPS)  12.6 us
    all_to_all x1, waiting for transfers between devices, exchange(): return lax.all_to_all(values, AXES, 0, 0, axis_index_groups=groups)  6.62 us
    pallas_call x4, Pallas kernels, call(): kernel_call(body, out_shape)  5.08 us
    all_to_all x1, starting transfers between devices, exchange(): return lax.all_to_all(values, AXES, 0, 0, axis_index_groups=groups)  4.06 us
    pallas_call x1, Pallas kernels, left_product(): kernel_call(left_body, (in_vmem(RANK, ROWS), in_vmem(ROWS, WIDTH)), in_sp...  2.69 us
    pallas_call x1, Pallas kernels, final(): kernel_call(final_body, (shape(ROWS, WIDTH), shape(RANK, WIDTH)), in_spec...  1.94 us
  transfers between devices with their start and end apart: 1, of which 1 were waited for; matrix products, arithmetic and copies ran while one was open for 0% of the time, Pallas kernels for 4%

profile of v9, /device:TPU:1, one launch (start us, length us, event | category | flops | bytes accessed | tf_op | source)
XLA Modules:
  0.0 79.5 jit_solution(6626416448932197610)
XLA Ops:
  0.7 2.7 %shard_map.58 = (f32[32,128]{1,0:T(8,128)S(1)}, f32[128,3584]{1,0:T(8,128)S(1)}) custom-call(bf16[128,3584]{1,0:T(8,128)(2,1)} %bitcast.13, f32[128,3584]{1,0:T(8,128)} %bitcast.12, f32[32,3584]{1,0:T(8,128)} %bitcast.14), custom_call_target="tpu_custom_call" | custom-call | tf_op jit(solution)/shard_map/pallas_call | solution.py:126
  3.4 0.1 iota.10.place_ref
  3.4 14.3 %all_to_all.20 = f32[8,32,128]{2,1,0:T(8,128)S(1)} all-to-all(f32[8,32,128]{2,1,0:T(8,128)S(1)} %broadcast_in_dim.14), channel_id=1, replica_groups={{0,256,64,320,128,384,192,448},{1,257,65,321,129,385,193,449},{2,258,66..., dimensions={0} | all-to-all | bytes 262144 | tf_op jit(solution)/shard_map/all_to_all | solution.py:245
  17.7 4.4 %all-gather = f32[64,128]{1,0:T(8,128)S(1)} all-gather(f32[32,128]{1,0:T(8,128)S(1)} %reduce_sum.9), channel_id=2, replica_groups={{0,32},{1,33},{2,34},{3,35},{4,36},{5,37},{6,38},{7,39},{8,40},{9,41},{..., dimensions={0}, use_global_device_ids=true | all-gather | bytes 49152 | tf_op jit(solution)/shard_map/all_gather | solution.py:253
  22.1 0.9 %shard_map.59 = (f32[2,32,16,128]{3,2,1,0:T(8,128)S(1)}, f32[32,128]{1,0:T(8,128)S(1)}) custom-call(f32[16,128]{1,0:T(8,128)S(1)} %iota.10.place_ref, f32[2,32,128]{2,1,0:T(8,128)S(1)} %bitcast.11, f32[128,3584]{1,0:T(8,128)S(1)} %get-tuple-element.19.merged_ref), custom_call_target="tpu_custom_call" | custom-call | tf_op jit(solution)/shard_map/pallas_call | solution.py:84
  23.0 2.2 %all_gather.18 = f32[2,32,16,128]{3,2,1,0:T(8,128)S(1)} all-gather(f32[1,32,16,128]{3,2,1,0:T(8,128)S(1)} %constant_dynamic-slice_fusion), channel_id=1, replica_groups={{0,32},{1,33},{2,34},{3,35},{4,36},{5,37},{6,38},{7,39},{8,40},{9,41},{..., dimensions={0}, use_global_device_ids=true | all-gather | bytes 786432 | tf_op jit(solution)/shard_map/all_gather | solution.py:253
  25.2 14.7 %all_to_all.21.parts_ref = f32[32,16,128]{2,1,0:T(8,128)S(1)} all-to-all(f32[32,16,128]{2,1,0:T(8,128)S(1)} %add_bitcast_fusion), channel_id=1, replica_groups={{0,4,8,12,16,20,24,28,2,6,10,14,18,22,26,30,1,5,9,13,17,21,25,29,3,7,11..., dimensions={0} | all-to-all | bytes 524288 | tf_op jit(solution)/shard_map/all_to_all | solution.py:245
  40.0 16.6 %all_to_all.22.parts_ref = f32[8,24,128]{2,1,0:T(8,128)S(1)} all-to-all(f32[8,24,128]{2,1,0:T(8,128)S(1)} %shard_map.60), channel_id=1, replica_groups={{0,256,64,320,128,384,192,448},{1,257,65,321,129,385,193,449},{2,258,66..., dimensions={0} | all-to-all | bytes 196608 | tf_op jit(solution)/shard_map/all_to_all | solution.py:245
  56.6 0.7 shard_map.61
  57.3 4.1 %all-to-all-start.3 = ((f32[32,16,128]{2,1,0:T(8,128)}), f32[32,16,128]{2,1,0:T(8,128)S(1)}, u32[]{:S(2)}, u32[]{:S(2)}) async-start(f32[32,16,128]{2,1,0:T(8,128)} %shard_map.61), calls=%async_computation.3 | async-start | bytes 524288 | tf_op jit(solution)/shard_map/all_to_all | solution.py:245
  61.4 3.5 %shard_map.62 = (f32[32,128]{1,0:T(8,128)}, bf16[128,192]{1,0:T(8,128)(2,1)S(1)}, bf16[32,192]{1,0:T(8,128)(2,1)S(1)}) custom-call(f32[8,24,128]{2,1,0:T(8,128)S(1)} %all_to_all.22.parts_ref, f32[32,128]{1,0:T(8,128)S(1)} %get-tuple-element.23.p_ref), custom_call_target="tpu_custom_call" | custom-call | tf_op jit(solution)/shard_map/pallas_call | solution.py:84
  64.9 6.6 %all-to-all-done.3 = f32[32,16,128]{2,1,0:T(8,128)S(1)} async-done(((f32[32,16,128]{2,1,0:T(8,128)}), f32[32,16,128]{2,1,0:T(8,128)S(1)}, u32[]{:S(2)}, u32[]{:S(2)}) %all-to-all-start.3) | async-done | bytes 262176 | tf_op jit(solution)/shard_map/all_to_all | solution.py:245
  71.5 6.1 %all-gather.1 = f32[64,16,128]{2,1,0:T(8,128)S(1)} all-gather(f32[32,16,128]{2,1,0:T(8,128)S(1)} %all-to-all-done.3), channel_id=3, replica_groups={{0,32},{1,33},{2,34},{3,35},{4,36},{5,37},{6,38},{7,39},{8,40},{9,41},{..., dimensions={0}, use_global_device_ids=true | all-gather | bytes 786432 | tf_op jit(solution)/shard_map/all_gather | solution.py:253
  77.5 1.9 %shard_map.63 = (f32[128,3584]{1,0:T(8,128)}, f32[32,3584]{1,0:T(8,128)}) custom-call(f32[2,32,16,128]{3,2,1,0:T(8,128)S(1)} %bitcast.10, bf16[32,192]{1,0:T(8,128)(2,1)S(1)} %get-tuple-element.24.inverse_ref, bf16[128,192]{1,0:T(8,128)(2,1)S(1)} %get-tuple-element.25.basis_ref, f32[128,3584]{1,0:T(8,128)S(1)} %get-tuple-element.19.merged_ref), custom_call_target="tpu_custom_call" | custom-call | tf_op jit(solution)/shard_map/pallas_call | solution.py:227
  (6 shorter events, 0.1 us)
Async XLA Ops:
  57.3 14.1 %all-to-all-start.3 = ((f32[32,16,128]{2,1,0:T(8,128)}), f32[32,16,128]{2,1,0:T(8,128)S(1)}, u32[]{:S(2)}, u32[]{:S(2)}) async-start(f32[32,16,128]{2,1,0:T(8,128)} %shard_map.61), calls=%async_computation.3 | async-start | bytes 524288 | tf_op jit(solution)/shard_map/all_to_all | solution.py:245

commit v10 on v7

--- a/solution.py
+++ b/solution.py
@@ -137,13 +137,17 @@
     )(*(pltpu.with_memory_space_constraint(value, pltpu.HBM) for value in (grad, error, q_rows)))
 
 
-def right_body(place_ref, parts_ref, merged_ref, pieces_ref, p_ref):
+def one_row():
+    return (lax.broadcasted_iota(jnp.int32, (8, LANES), 0) == lax.axis_index("dp") // 2).astype(F32)
+
+
+def right_body(parts_ref, merged_ref, pieces_ref, p_ref):
     p_sum = jnp.sum(parts_ref[...], axis=0)
     p_ref[...] = p_sum
     p_parts = jnp.concatenate(split3(p_sum), axis=0)
     gram = lax.dot_general(p_sum, p_sum, NT, precision=HIGHEST, preferred_element_type=F32)
     packed = jnp.concatenate([gram[8 * a : 8 * a + 8] for a in range(4)], axis=1)
-    row = 0.5 * jnp.sum(packed * place_ref[:8, :], axis=0, keepdims=True)
+    row = 0.5 * jnp.sum(packed * one_row(), axis=0, keepdims=True)
     for half in range(2):
         h, m, l = split3(merged_ref[:, half * HALF : (half + 1) * HALF])
         with_h = dot(p_parts, h)
@@ -157,11 +161,11 @@
         pieces_ref[half, :, TILES + 1, :] = jnp.zeros((RANK, LANES), F32)
 
 
-def right_product(place, parts, merged):
-    return vmem_call(right_body, (in_vmem(2, RANK, PIECE, LANES), in_vmem(RANK, ROWS)))(place, parts, merged)
-
-
-def plane_body(place_ref, parts_ref, out_ref):
+def right_product(parts, merged):
+    return vmem_call(right_body, (in_vmem(2, RANK, PIECE, LANES), in_vmem(RANK, ROWS)))(parts, merged)
+
+
+def plane_body(parts_ref, out_ref):
     rows = parts_ref[0]
     for member in range(1, PLANE):
         rows += parts_ref[member]
@@ -169,7 +173,7 @@
     total = apart[FAR_FIRST[0]]
     for z in FAR_FIRST[1:]:
         total += apart[z]
-    gram = jnp.where(place_ref[8:, :] > 0, total * place_ref[:8, :], jnp.concatenate(apart, axis=0))
+    gram = jnp.where(lax.axis_index("dp") % 2 == 0, total * one_row(), jnp.concatenate(apart, axis=0))
     both = jnp.concatenate([rows, gram], axis=0)
     for member in range(RING):
         out_ref[member] = both
@@ -257,17 +261,14 @@
     replicas = lax.axis_size("dp")
     dp = lax.axis_index("dp").astype(jnp.uint32)
     core = dp % 2
-    row = lax.broadcasted_iota(jnp.uint32, (16, LANES), 0)
-    place = jnp.where(row < 8, row == dp // 2, core == 0).astype(F32)
-
     p_local, merged = left_product(grad[0], error[0], q_prev.T)
-    p_both, place, core, other = lax.optimization_barrier((both_cores(p_local), place, core, 1 - core))
+    p_both, core, other = lax.optimization_barrier((both_cores(p_local), core, 1 - core))
     p_parts = spread(jnp.sum(p_both, axis=0), Y_GROUPS)
 
-    pieces, p_sum = right_product(place, p_parts, merged)
+    pieces, p_sum = right_product(p_parts, merged)
     traded = both_cores(pick(pieces, other))
     pieces = exchange(pick(pieces, core) + pick(traded, other), PLANE_GROUPS)
-    lines = vmem_call(plane_body, in_vmem(RING, PIECE + 8, LANES))(place, pieces)
+    lines = vmem_call(plane_body, in_vmem(RING, PIECE + 8, LANES))(pieces)
     lines = exchange(lines, LINE_GROUPS)
     own = vmem_call(line_body, in_vmem(PLANE, PIECE, LANES))(lines)
     own = exchange(own, PLANE_GROUPS)

time: 80 us -> 79.9 us (level)
  no operation moved by 1% of the time
where the time goes in v10:
time: 79.9 us; the launch traced here: 79.5 us
  blocking collectives  58.4 us (73%)
  Pallas kernels  9.7 us (12%)
  waiting for transfers between devices  6.59 us (8%)
  starting transfers between devices  4.13 us (5%)
    all_to_all x3, blocking collectives, exchange(): return lax.all_to_all(values, AXES, 0, 0, axis_index_groups=groups)  40.4 us
    all_gather x3, blocking collectives, both_cores(): return lax.all_gather(value, AXES, axis_index_groups=CHIP_GROUPS)  18 us
    all_to_all x1, waiting for transfers between devices, exchange(): return lax.all_to_all(values, AXES, 0, 0, axis_index_groups=groups)  6.59 us
    pallas_call x4, Pallas kernels, call(): kernel_call(body, out_shape)  5.07 us
    all_to_all x1, starting transfers between devices, exchange(): return lax.all_to_all(values, AXES, 0, 0, axis_index_groups=groups)  4.13 us
    pallas_call x1, Pallas kernels, left_product(): kernel_call(left_body, (in_vmem(RANK, ROWS), in_vmem(ROWS, WIDTH)), in_sp...  2.69 us
    pallas_call x1, Pallas kernels, final(): kernel_call(final_body, (shape(ROWS, WIDTH), shape(RANK, WIDTH)), in_spec...  1.94 us
  transfers between devices with their start and end apart: 1, of which 1 were waited for; matrix products, arithmetic and copies ran while one was open for 0% of the time, Pallas kernels for 4%

profile of v10, /device:TPU:1, one launch (start us, length us, event | category | flops | bytes accessed | tf_op | source)
XLA Modules:
  0.0 79.5 jit_solution(15192347726144343548)
XLA Ops:
  0.6 2.7 %shard_map.58 = (f32[32,128]{1,0:T(8,128)S(1)}, f32[128,3584]{1,0:T(8,128)S(1)}) custom-call(bf16[128,3584]{1,0:T(8,128)(2,1)} %bitcast.12, f32[128,3584]{1,0:T(8,128)} %bitcast.11, f32[32,3584]{1,0:T(8,128)} %bitcast.13), custom_call_target="tpu_custom_call" | custom-call | tf_op jit(solution)/shard_map/pallas_call | solution.py:126
  3.3 8.4 %all-gather = f32[64,128]{1,0:T(8,128)S(1)} all-gather(f32[32,128]{1,0:T(8,128)S(1)} %get-tuple-element.15), channel_id=2, replica_groups={{0,32},{1,33},{2,34},{3,35},{4,36},{5,37},{6,38},{7,39},{8,40},{9,41},{..., dimensions={0}, use_global_device_ids=true | all-gather | bytes 49152 | tf_op jit(solution)/shard_map/all_gather | solution.py:257
  11.7 9.2 %all_to_all.20.parts_ref = f32[8,32,128]{2,1,0:T(8,128)S(1)} all-to-all(f32[8,32,128]{2,1,0:T(8,128)S(1)} %broadcast_in_dim.4), channel_id=1, replica_groups={{0,256,64,320,128,384,192,448},{1,257,65,321,129,385,193,449},{2,258,66..., dimensions={0} | all-to-all | bytes 262144 | tf_op jit(solution)/shard_map/all_to_all | solution.py:249
  20.9 0.8 %shard_map.59 = (f32[2,32,16,128]{3,2,1,0:T(8,128)S(1)}, f32[32,128]{1,0:T(8,128)S(1)}) custom-call(f32[8,32,128]{2,1,0:T(8,128)S(1)} %all_to_all.20.parts_ref, f32[128,3584]{1,0:T(8,128)S(1)} %get-tuple-element.17.merged_ref), custom_call_target="tpu_custom_call" | custom-call | tf_op jit(solution)/shard_map/pallas_call | solution.py:84
  21.8 3.5 %all_gather.18 = f32[2,32,16,128]{3,2,1,0:T(8,128)S(1)} all-gather(f32[1,32,16,128]{3,2,1,0:T(8,128)S(1)} %constant_dynamic-slice_fusion), channel_id=1, replica_groups={{0,32},{1,33},{2,34},{3,35},{4,36},{5,37},{6,38},{7,39},{8,40},{9,41},{..., dimensions={0}, use_global_device_ids=true | all-gather | bytes 786432 | tf_op jit(solution)/shard_map/all_gather | solution.py:257
  25.3 14.6 %all_to_all.21.parts_ref = f32[32,16,128]{2,1,0:T(8,128)S(1)} all-to-all(f32[32,16,128]{2,1,0:T(8,128)S(1)} %add_bitcast_fusion), channel_id=1, replica_groups={{0,4,8,12,16,20,24,28,2,6,10,14,18,22,26,30,1,5,9,13,17,21,25,29,3,7,11..., dimensions={0} | all-to-all | bytes 524288 | tf_op jit(solution)/shard_map/all_to_all | solution.py:249
  40.0 16.6 %all_to_all.22.parts_ref = f32[8,24,128]{2,1,0:T(8,128)S(1)} all-to-all(f32[8,24,128]{2,1,0:T(8,128)S(1)} %shard_map.60), channel_id=1, replica_groups={{0,256,64,320,128,384,192,448},{1,257,65,321,129,385,193,449},{2,258,66..., dimensions={0} | all-to-all | bytes 196608 | tf_op jit(solution)/shard_map/all_to_all | solution.py:249
  56.6 0.7 shard_map.61
  57.3 4.1 %all-to-all-start.3 = ((f32[32,16,128]{2,1,0:T(8,128)}), f32[32,16,128]{2,1,0:T(8,128)S(1)}, u32[]{:S(2)}, u32[]{:S(2)}) async-start(f32[32,16,128]{2,1,0:T(8,128)} %shard_map.61), calls=%async_computation.3 | async-start | bytes 524288 | tf_op jit(solution)/shard_map/all_to_all | solution.py:249
  61.4 3.5 %shard_map.62 = (f32[32,128]{1,0:T(8,128)}, bf16[128,192]{1,0:T(8,128)(2,1)S(1)}, bf16[32,192]{1,0:T(8,128)(2,1)S(1)}) custom-call(f32[8,24,128]{2,1,0:T(8,128)S(1)} %all_to_all.22.parts_ref, f32[32,128]{1,0:T(8,128)S(1)} %get-tuple-element.21.p_ref), custom_call_target="tpu_custom_call" | custom-call | tf_op jit(solution)/shard_map/pallas_call | solution.py:84
  64.9 6.6 %all-to-all-done.3 = f32[32,16,128]{2,1,0:T(8,128)S(1)} async-done(((f32[32,16,128]{2,1,0:T(8,128)}), f32[32,16,128]{2,1,0:T(8,128)S(1)}, u32[]{:S(2)}, u32[]{:S(2)}) %all-to-all-start.3) | async-done | bytes 262176 | tf_op jit(solution)/shard_map/all_to_all | solution.py:249
  71.5 6.1 %all-gather.1 = f32[64,16,128]{2,1,0:T(8,128)S(1)} all-gather(f32[32,16,128]{2,1,0:T(8,128)S(1)} %all-to-all-done.3), channel_id=3, replica_groups={{0,32},{1,33},{2,34},{3,35},{4,36},{5,37},{6,38},{7,39},{8,40},{9,41},{..., dimensions={0}, use_global_device_ids=true | all-gather | bytes 786432 | tf_op jit(solution)/shard_map/all_gather | solution.py:257
  77.6 1.9 %shard_map.63 = (f32[128,3584]{1,0:T(8,128)}, f32[32,3584]{1,0:T(8,128)}) custom-call(f32[2,32,16,128]{3,2,1,0:T(8,128)S(1)} %bitcast.10, bf16[32,192]{1,0:T(8,128)(2,1)S(1)} %get-tuple-element.22.inverse_ref, bf16[128,192]{1,0:T(8,128)(2,1)S(1)} %get-tuple-element.23.basis_ref, f32[128,3584]{1,0:T(8,128)S(1)} %get-tuple-element.17.merged_ref), custom_call_target="tpu_custom_call" | custom-call | tf_op jit(solution)/shard_map/pallas_call | solution.py:231
  (5 shorter events, 0.1 us)
Async XLA Ops:
  57.3 14.2 %all-to-all-start.3 = ((f32[32,16,128]{2,1,0:T(8,128)}), f32[32,16,128]{2,1,0:T(8,128)S(1)}, u32[]{:S(2)}, u32[]{:S(2)}) async-start(f32[32,16,128]{2,1,0:T(8,128)} %shard_map.61), calls=%async_computation.3 | async-start | bytes 524288 | tf_op jit(solution)/shard_map/all_to_all | solution.py:249
